TPU v7x, 128 devices: a whole 4x4x4 slice. The times are simulated.
128 devices in a mesh: rows: 8 (over y_lo, x), blk: 16 (over y_hi, z, core).
Axes of the slice: x: 4, y: 4 (y_hi: 2, y_lo: 2; y = y_hi * 2 + y_lo), z: 4, core: 2. Of those that a mesh axis runs over, the one named last changes fastest.
Arguments:
- points: float32 [3, 262144], P(None, ('rows', 'blk')), may hold values from -6 to 6
- normals: float32 [3, 16384], P(None, ('rows', 'blk')), may hold values from -1 to 1
- weights: float32 [262144], P(('rows', 'blk')), may hold values from 0.25 to 1
- visible: int32 [512, 64], P(('rows', 'blk')), may hold values 0 or 1
- quad_mask: int32 [512, 64], P(('rows', 'blk')), may hold values from 1 to 65535
- owners: int32 [128, 256, 1], P(('rows', 'blk')), may hold values from 0 to 127; in each aligned block of 256 rows (0 to 255, 256 to 511, ..., all dimensions but the last counted through in order) at most 4 rows name the same one
Outputs:
- received: float32 [65536, 1024], P(('rows', 'blk'))
Inputs may be any that keep to these rules, and one draw needn't show every extreme that they name: `owners`: among the 256 tiles of one device no owner is named more than 4 times, a bound that some block reaches.
All inputs are finite; a program needn't handle non-finite values. No bound on the sum of `visible` on one device may be relied on, other than what follows from the above.
Results may differ from a plain program's by a relative error of at most 0.0003.
Values sent between devices are 32-bit elements; how exact they have to be, the bound alone decides.
No kernel may reach another device: no remote copies, remote signals or barrier semaphores. Data moves between devices by JAX's collectives and lax.ppermute only.
A program may use at most 64 MiB of HBM per device.

v0:
```python
import math

import jax
import jax.numpy as jnp
from jax import lax
from jax.sharding import PartitionSpec as P

Q = 16
TS = 32


softening = 0.05


def passed_along(block, axis, distance):
    devices = range(lax.axis_size(axis))
    route = [((i - distance) % len(devices), i) for i in devices]
    return lax.ppermute(block, axis, route)


def tile_bits(quad_mask):
    shifts = jnp.arange(Q, dtype=jnp.int32)
    return (quad_mask[..., None] >> shifts & 1).astype(jnp.float32)


def row_block(
    row_points, row_normals, row_weights, col_points, col_normals, col_weights, bits, seen
):
    rows = row_normals.shape[1]
    patches = col_normals.shape[1]
    row_vecs = jnp.repeat(row_normals, Q, axis=1)
    col_vecs = jnp.repeat(col_normals, Q, axis=1)
    delta_x = col_points[0][None, :] - row_points[0][:, None]
    delta_y = col_points[1][None, :] - row_points[1][:, None]
    delta_z = col_points[2][None, :] - row_points[2][:, None]
    distance = delta_x * delta_x + delta_y * delta_y + delta_z * delta_z + softening
    cos_row = (
        row_vecs[0][:, None] * delta_x
        + row_vecs[1][:, None] * delta_y
        + row_vecs[2][:, None] * delta_z
    )
    cos_col = -(
        col_vecs[0][None, :] * delta_x
        + col_vecs[1][None, :] * delta_y
        + col_vecs[2][None, :] * delta_z
    )
    kernel = jnp.maximum(cos_row, 0.0) * jnp.maximum(cos_col, 0.0) / (math.pi * distance * distance)
    kernel = kernel * col_weights[None, :]
    summed = jnp.sum(kernel.reshape(rows * Q, patches, Q), axis=2).reshape(rows, Q, patches)
    quad_weights = row_weights.reshape(rows, Q)
    active = jnp.repeat(jnp.repeat(bits.transpose(0, 2, 1), TS, axis=0), TS, axis=2)
    seen_full = jnp.repeat(jnp.repeat(seen, TS, axis=0), TS, axis=1)
    folded = jnp.sum(summed * quad_weights[:, :, None] * active, axis=1)
    area = jnp.sum(quad_weights, axis=1)
    return folded / area[:, None] * seen_full


def to_tiles(factors):
    height, width = factors.shape
    blocks = factors.reshape(height // TS, TS, width // TS, TS).transpose(0, 2, 1, 3)
    return blocks.reshape(-1, TS * TS)


def owner_slots(targets, tiles, owner_count, capacity):
    same_owner = targets[:, None] == targets[None, :]
    order = jnp.arange(targets.shape[0], dtype=jnp.int32)
    earlier = order[:, None] > order[None, :]
    rank = jnp.sum((same_owner & earlier).astype(jnp.int32), axis=1)
    slot = targets * capacity + rank
    empty = jnp.zeros((owner_count * capacity, tiles.shape[1]), tiles.dtype)
    return empty.at[slot].set(tiles)


def pack_block(points, normals, weights):
    return jnp.concatenate([points.reshape(-1), weights, normals.reshape(-1)])


def unpack_block(flat, point_count, patch_count):
    points = flat[: 3 * point_count].reshape(3, point_count)
    weights = flat[3 * point_count : 4 * point_count]
    normals = flat[4 * point_count :].reshape(3, patch_count)
    return (points, normals, weights)


def forward(flat):
    return passed_along(flat, "blk", 1)


def on_device(points, normals, weights, visible, quad_mask, owners):
    loop_len = lax.axis_size("blk")
    row_len = lax.axis_size("rows")
    devices = row_len * loop_len
    here = lax.axis_index("blk")
    point_count = points.shape[1]
    patch_count = normals.shape[1]
    span = patch_count // TS
    bits = tile_bits(quad_mask)
    seen = visible.astype(jnp.float32)

    def place(factors, flat, source):
        col_points, col_normals, col_weights = unpack_block(flat, point_count, patch_count)
        block_bits = lax.dynamic_slice_in_dim(bits, source * span, span, 1)
        block_seen = lax.dynamic_slice_in_dim(seen, source * span, span, 1)
        block = row_block(
            points, normals, weights, col_points, col_normals, col_weights, block_bits, block_seen
        )
        return lax.dynamic_update_slice_in_dim(factors, block, source * patch_count, 1)

    own_block = pack_block(points, normals, weights)
    factors = jnp.zeros((patch_count, loop_len * patch_count), jnp.float32)

    def one_turn(turn, carry):
        factors, flat = carry
        factors = place(factors, flat, (here - turn) % loop_len)
        return (factors, forward(flat))

    factors, flat = lax.fori_loop(0, loop_len - 1, one_turn, (factors, own_block))
    factors = place(factors, flat, (here - loop_len + 1) % loop_len)
    tiles = to_tiles(factors)
    capacity = max(2, 2 * tiles.shape[0] // devices)
    outgoing = owner_slots(owners[0, :, 0], tiles, devices, capacity)
    arrived = lax.all_to_all(outgoing, ("rows", "blk"), split_axis=0, concat_axis=0, tiled=True)
    return arrived


def solution(mesh):
    placed = (
        P(None, ("rows", "blk")),
        P(None, ("rows", "blk")),
        P(("rows", "blk")),
        P(("rows", "blk"), None),
        P(("rows", "blk"), None),
        P(("rows", "blk"), None, None),
    )
    return jax.shard_map(
        on_device, mesh=mesh, in_specs=placed, out_specs=P(("rows", "blk"), None), check_vma=False
    )
```

profile of v0, /device:TPU:1, one launch (start us, length us, event | category | flops | bytes accessed | tf_op | source)
XLA Modules:
  0.0 606.8 jit_solution(16235709720811665652)
XLA Ops:
  4.0 514.8 %while.17 = (s32[]{:T(128)}, f32[128,2048]{0,1:T(8,128)S(1)}, f32[8576]{0:T(1024)S(1)}, f32[3,128]{1,0:T(4,128)}, f32[3,2048]{1,0:T(4,128)}, /*index=5*/f32[2048...) while((s32[]{:T(128)}, f32[128,2048]{0,1:T(8,128)S(1)}, ...), condition=%wide.region_5.6_spmd, body=%wide.region_2.5_spmd.sunk | while | flops 117981208 | bytes 5273738 | solution.py:117
  4.0 3.1 collective-permute-start
  9.9 19.2 %fusion.44 = f32[2048,128]{1,0:T(8,128)S(1)} fusion(f32[128,16]{0,1:T(8,128)S(1)} %copy.39, f32[128]{0:T(128)S(1)} %get-tuple-element.356, f32[128]{0:T(128)S(1)} %get-tuple-element.357, f32[128]{0:T(128)S(1)} %get-tuple-element.358, f32[2048]{0:T(1024)S(1)} %bitcast.67, f32[128,16]{0,1:T(8,128)S(1)} %copy.40, f32[2048]{0:T(1024)S(1)} %broadcast_in_dim.133, ...), kind=kLoop, calls=%fused_computation.24.clone.1 | loop fusion | flops 117178368 | bytes 1132032 | tf_op jit(solution)/shard_map/while/body/eval_jaxpr/reduce_sum | solution.py:49
  29.1 3.2 reshape.484
  32.6 7.4 %multiply_reduce_fusion.3 = f32[128,4,32]{2,1,0:T(4,128)S(1)} fusion(f32[128,16,4,32]{3,2,1,0:T(4,128)} %reshape.484, f32[128,16,4]{2,1,0:T(8,128)S(1)} %bitcast.63, f32[128,16]{1,0:T(8,128)S(1)} %mul.706), kind=kLoop, calls=%fused_computation.25.clone.1 | loop fusion | flops 770048 | bytes 1155072 | tf_op jit(solution)/shard_map/while/body/eval_jaxpr/reduce_sum | solution.py:53
  43.4 19.2 %fusion.44 = f32[2048,128]{1,0:T(8,128)S(1)} fusion(f32[128,16]{0,1:T(8,128)S(1)} %copy.39, f32[128]{0:T(128)S(1)} %get-tuple-element.356, f32[128]{0:T(128)S(1)} %get-tuple-element.357, f32[128]{0:T(128)S(1)} %get-tuple-element.358, f32[2048]{0:T(1024)S(1)} %bitcast.67, f32[128,16]{0,1:T(8,128)S(1)} %copy.40, f32[2048]{0:T(1024)S(1)} %broadcast_in_dim.133, ...), kind=kLoop, calls=%fused_computation.24.clone.1 | loop fusion | flops 117178368 | bytes 1132032 | tf_op jit(solution)/shard_map/while/body/eval_jaxpr/reduce_sum | solution.py:49
  62.6 3.2 reshape.484
  66.0 7.4 %multiply_reduce_fusion.3 = f32[128,4,32]{2,1,0:T(4,128)S(1)} fusion(f32[128,16,4,32]{3,2,1,0:T(4,128)} %reshape.484, f32[128,16,4]{2,1,0:T(8,128)S(1)} %bitcast.63, f32[128,16]{1,0:T(8,128)S(1)} %mul.706), kind=kLoop, calls=%fused_computation.25.clone.1 | loop fusion | flops 770048 | bytes 1155072 | tf_op jit(solution)/shard_map/while/body/eval_jaxpr/reduce_sum | solution.py:53
  73.8 2.0 collective-permute-start
  78.7 19.2 %fusion.44 = f32[2048,128]{1,0:T(8,128)S(1)} fusion(f32[128,16]{0,1:T(8,128)S(1)} %copy.39, f32[128]{0:T(128)S(1)} %get-tuple-element.356, f32[128]{0:T(128)S(1)} %get-tuple-element.357, f32[128]{0:T(128)S(1)} %get-tuple-element.358, f32[2048]{0:T(1024)S(1)} %bitcast.67, f32[128,16]{0,1:T(8,128)S(1)} %copy.40, f32[2048]{0:T(1024)S(1)} %broadcast_in_dim.133, ...), kind=kLoop, calls=%fused_computation.24.clone.1 | loop fusion | flops 117178368 | bytes 1132032 | tf_op jit(solution)/shard_map/while/body/eval_jaxpr/reduce_sum | solution.py:49
  97.9 3.2 reshape.484
  101.3 7.4 %multiply_reduce_fusion.3 = f32[128,4,32]{2,1,0:T(4,128)S(1)} fusion(f32[128,16,4,32]{3,2,1,0:T(4,128)} %reshape.484, f32[128,16,4]{2,1,0:T(8,128)S(1)} %bitcast.63, f32[128,16]{1,0:T(8,128)S(1)} %mul.706), kind=kLoop, calls=%fused_computation.25.clone.1 | loop fusion | flops 770048 | bytes 1155072 | tf_op jit(solution)/shard_map/while/body/eval_jaxpr/reduce_sum | solution.py:53
  112.1 19.2 %fusion.44 = f32[2048,128]{1,0:T(8,128)S(1)} fusion(f32[128,16]{0,1:T(8,128)S(1)} %copy.39, f32[128]{0:T(128)S(1)} %get-tuple-element.356, f32[128]{0:T(128)S(1)} %get-tuple-element.357, f32[128]{0:T(128)S(1)} %get-tuple-element.358, f32[2048]{0:T(1024)S(1)} %bitcast.67, f32[128,16]{0,1:T(8,128)S(1)} %copy.40, f32[2048]{0:T(1024)S(1)} %broadcast_in_dim.133, ...), kind=kLoop, calls=%fused_computation.24.clone.1 | loop fusion | flops 117178368 | bytes 1132032 | tf_op jit(solution)/shard_map/while/body/eval_jaxpr/reduce_sum | solution.py:49
  131.3 3.2 reshape.484
  134.7 7.4 %multiply_reduce_fusion.3 = f32[128,4,32]{2,1,0:T(4,128)S(1)} fusion(f32[128,16,4,32]{3,2,1,0:T(4,128)} %reshape.484, f32[128,16,4]{2,1,0:T(8,128)S(1)} %bitcast.63, f32[128,16]{1,0:T(8,128)S(1)} %mul.706), kind=kLoop, calls=%fused_computation.25.clone.1 | loop fusion | flops 770048 | bytes 1155072 | tf_op jit(solution)/shard_map/while/body/eval_jaxpr/reduce_sum | solution.py:53
  142.5 1.7 collective-permute-start
  147.1 19.2 %fusion.44 = f32[2048,128]{1,0:T(8,128)S(1)} fusion(f32[128,16]{0,1:T(8,128)S(1)} %copy.39, f32[128]{0:T(128)S(1)} %get-tuple-element.356, f32[128]{0:T(128)S(1)} %get-tuple-element.357, f32[128]{0:T(128)S(1)} %get-tuple-element.358, f32[2048]{0:T(1024)S(1)} %bitcast.67, f32[128,16]{0,1:T(8,128)S(1)} %copy.40, f32[2048]{0:T(1024)S(1)} %broadcast_in_dim.133, ...), kind=kLoop, calls=%fused_computation.24.clone.1 | loop fusion | flops 117178368 | bytes 1132032 | tf_op jit(solution)/shard_map/while/body/eval_jaxpr/reduce_sum | solution.py:49
  166.3 3.2 reshape.484
  169.7 7.4 %multiply_reduce_fusion.3 = f32[128,4,32]{2,1,0:T(4,128)S(1)} fusion(f32[128,16,4,32]{3,2,1,0:T(4,128)} %reshape.484, f32[128,16,4]{2,1,0:T(8,128)S(1)} %bitcast.63, f32[128,16]{1,0:T(8,128)S(1)} %mul.706), kind=kLoop, calls=%fused_computation.25.clone.1 | loop fusion | flops 770048 | bytes 1155072 | tf_op jit(solution)/shard_map/while/body/eval_jaxpr/reduce_sum | solution.py:53
  180.5 19.2 %fusion.44 = f32[2048,128]{1,0:T(8,128)S(1)} fusion(f32[128,16]{0,1:T(8,128)S(1)} %copy.39, f32[128]{0:T(128)S(1)} %get-tuple-element.356, f32[128]{0:T(128)S(1)} %get-tuple-element.357, f32[128]{0:T(128)S(1)} %get-tuple-element.358, f32[2048]{0:T(1024)S(1)} %bitcast.67, f32[128,16]{0,1:T(8,128)S(1)} %copy.40, f32[2048]{0:T(1024)S(1)} %broadcast_in_dim.133, ...), kind=kLoop, calls=%fused_computation.24.clone.1 | loop fusion | flops 117178368 | bytes 1132032 | tf_op jit(solution)/shard_map/while/body/eval_jaxpr/reduce_sum | solution.py:49
  199.7 3.2 reshape.484
  203.1 7.4 %multiply_reduce_fusion.3 = f32[128,4,32]{2,1,0:T(4,128)S(1)} fusion(f32[128,16,4,32]{3,2,1,0:T(4,128)} %reshape.484, f32[128,16,4]{2,1,0:T(8,128)S(1)} %bitcast.63, f32[128,16]{1,0:T(8,128)S(1)} %mul.706), kind=kLoop, calls=%fused_computation.25.clone.1 | loop fusion | flops 770048 | bytes 1155072 | tf_op jit(solution)/shard_map/while/body/eval_jaxpr/reduce_sum | solution.py:53
  210.9 1.9 collective-permute-start
  215.7 19.2 %fusion.44 = f32[2048,128]{1,0:T(8,128)S(1)} fusion(f32[128,16]{0,1:T(8,128)S(1)} %copy.39, f32[128]{0:T(128)S(1)} %get-tuple-element.356, f32[128]{0:T(128)S(1)} %get-tuple-element.357, f32[128]{0:T(128)S(1)} %get-tuple-element.358, f32[2048]{0:T(1024)S(1)} %bitcast.67, f32[128,16]{0,1:T(8,128)S(1)} %copy.40, f32[2048]{0:T(1024)S(1)} %broadcast_in_dim.133, ...), kind=kLoop, calls=%fused_computation.24.clone.1 | loop fusion | flops 117178368 | bytes 1132032 | tf_op jit(solution)/shard_map/while/body/eval_jaxpr/reduce_sum | solution.py:49
  234.9 3.2 reshape.484
  238.3 7.4 %multiply_reduce_fusion.3 = f32[128,4,32]{2,1,0:T(4,128)S(1)} fusion(f32[128,16,4,32]{3,2,1,0:T(4,128)} %reshape.484, f32[128,16,4]{2,1,0:T(8,128)S(1)} %bitcast.63, f32[128,16]{1,0:T(8,128)S(1)} %mul.706), kind=kLoop, calls=%fused_computation.25.clone.1 | loop fusion | flops 770048 | bytes 1155072 | tf_op jit(solution)/shard_map/while/body/eval_jaxpr/reduce_sum | solution.py:53
  249.1 19.2 %fusion.44 = f32[2048,128]{1,0:T(8,128)S(1)} fusion(f32[128,16]{0,1:T(8,128)S(1)} %copy.39, f32[128]{0:T(128)S(1)} %get-tuple-element.356, f32[128]{0:T(128)S(1)} %get-tuple-element.357, f32[128]{0:T(128)S(1)} %get-tuple-element.358, f32[2048]{0:T(1024)S(1)} %bitcast.67, f32[128,16]{0,1:T(8,128)S(1)} %copy.40, f32[2048]{0:T(1024)S(1)} %broadcast_in_dim.133, ...), kind=kLoop, calls=%fused_computation.24.clone.1 | loop fusion | flops 117178368 | bytes 1132032 | tf_op jit(solution)/shard_map/while/body/eval_jaxpr/reduce_sum | solution.py:49
  268.3 3.2 reshape.484
  271.7 7.4 %multiply_reduce_fusion.3 = f32[128,4,32]{2,1,0:T(4,128)S(1)} fusion(f32[128,16,4,32]{3,2,1,0:T(4,128)} %reshape.484, f32[128,16,4]{2,1,0:T(8,128)S(1)} %bitcast.63, f32[128,16]{1,0:T(8,128)S(1)} %mul.706), kind=kLoop, calls=%fused_computation.25.clone.1 | loop fusion | flops 770048 | bytes 1155072 | tf_op jit(solution)/shard_map/while/body/eval_jaxpr/reduce_sum | solution.py:53
  279.5 2.0 collective-permute-start
  284.4 19.2 %fusion.44 = f32[2048,128]{1,0:T(8,128)S(1)} fusion(f32[128,16]{0,1:T(8,128)S(1)} %copy.39, f32[128]{0:T(128)S(1)} %get-tuple-element.356, f32[128]{0:T(128)S(1)} %get-tuple-element.357, f32[128]{0:T(128)S(1)} %get-tuple-element.358, f32[2048]{0:T(1024)S(1)} %bitcast.67, f32[128,16]{0,1:T(8,128)S(1)} %copy.40, f32[2048]{0:T(1024)S(1)} %broadcast_in_dim.133, ...), kind=kLoop, calls=%fused_computation.24.clone.1 | loop fusion | flops 117178368 | bytes 1132032 | tf_op jit(solution)/shard_map/while/body/eval_jaxpr/reduce_sum | solution.py:49
  303.6 3.2 reshape.484
  307.0 7.4 %multiply_reduce_fusion.3 = f32[128,4,32]{2,1,0:T(4,128)S(1)} fusion(f32[128,16,4,32]{3,2,1,0:T(4,128)} %reshape.484, f32[128,16,4]{2,1,0:T(8,128)S(1)} %bitcast.63, f32[128,16]{1,0:T(8,128)S(1)} %mul.706), kind=kLoop, calls=%fused_computation.25.clone.1 | loop fusion | flops 770048 | bytes 1155072 | tf_op jit(solution)/shard_map/while/body/eval_jaxpr/reduce_sum | solution.py:53
  317.8 19.2 %fusion.44 = f32[2048,128]{1,0:T(8,128)S(1)} fusion(f32[128,16]{0,1:T(8,128)S(1)} %copy.39, f32[128]{0:T(128)S(1)} %get-tuple-element.356, f32[128]{0:T(128)S(1)} %get-tuple-element.357, f32[128]{0:T(128)S(1)} %get-tuple-element.358, f32[2048]{0:T(1024)S(1)} %bitcast.67, f32[128,16]{0,1:T(8,128)S(1)} %copy.40, f32[2048]{0:T(1024)S(1)} %broadcast_in_dim.133, ...), kind=kLoop, calls=%fused_computation.24.clone.1 | loop fusion | flops 117178368 | bytes 1132032 | tf_op jit(solution)/shard_map/while/body/eval_jaxpr/reduce_sum | solution.py:49
  337.0 3.2 reshape.484
  340.4 7.4 %multiply_reduce_fusion.3 = f32[128,4,32]{2,1,0:T(4,128)S(1)} fusion(f32[128,16,4,32]{3,2,1,0:T(4,128)} %reshape.484, f32[128,16,4]{2,1,0:T(8,128)S(1)} %bitcast.63, f32[128,16]{1,0:T(8,128)S(1)} %mul.706), kind=kLoop, calls=%fused_computation.25.clone.1 | loop fusion | flops 770048 | bytes 1155072 | tf_op jit(solution)/shard_map/while/body/eval_jaxpr/reduce_sum | solution.py:53
  348.3 2.0 collective-permute-start
  353.1 19.2 %fusion.44 = f32[2048,128]{1,0:T(8,128)S(1)} fusion(f32[128,16]{0,1:T(8,128)S(1)} %copy.39, f32[128]{0:T(128)S(1)} %get-tuple-element.356, f32[128]{0:T(128)S(1)} %get-tuple-element.357, f32[128]{0:T(128)S(1)} %get-tuple-element.358, f32[2048]{0:T(1024)S(1)} %bitcast.67, f32[128,16]{0,1:T(8,128)S(1)} %copy.40, f32[2048]{0:T(1024)S(1)} %broadcast_in_dim.133, ...), kind=kLoop, calls=%fused_computation.24.clone.1 | loop fusion | flops 117178368 | bytes 1132032 | tf_op jit(solution)/shard_map/while/body/eval_jaxpr/reduce_sum | solution.py:49
  372.3 3.2 reshape.484
  375.7 7.4 %multiply_reduce_fusion.3 = f32[128,4,32]{2,1,0:T(4,128)S(1)} fusion(f32[128,16,4,32]{3,2,1,0:T(4,128)} %reshape.484, f32[128,16,4]{2,1,0:T(8,128)S(1)} %bitcast.63, f32[128,16]{1,0:T(8,128)S(1)} %mul.706), kind=kLoop, calls=%fused_computation.25.clone.1 | loop fusion | flops 770048 | bytes 1155072 | tf_op jit(solution)/shard_map/while/body/eval_jaxpr/reduce_sum | solution.py:53
  386.5 19.2 %fusion.44 = f32[2048,128]{1,0:T(8,128)S(1)} fusion(f32[128,16]{0,1:T(8,128)S(1)} %copy.39, f32[128]{0:T(128)S(1)} %get-tuple-element.356, f32[128]{0:T(128)S(1)} %get-tuple-element.357, f32[128]{0:T(128)S(1)} %get-tuple-element.358, f32[2048]{0:T(1024)S(1)} %bitcast.67, f32[128,16]{0,1:T(8,128)S(1)} %copy.40, f32[2048]{0:T(1024)S(1)} %broadcast_in_dim.133, ...), kind=kLoop, calls=%fused_computation.24.clone.1 | loop fusion | flops 117178368 | bytes 1132032 | tf_op jit(solution)/shard_map/while/body/eval_jaxpr/reduce_sum | solution.py:49
  405.7 3.2 reshape.484
  409.2 7.4 %multiply_reduce_fusion.3 = f32[128,4,32]{2,1,0:T(4,128)S(1)} fusion(f32[128,16,4,32]{3,2,1,0:T(4,128)} %reshape.484, f32[128,16,4]{2,1,0:T(8,128)S(1)} %bitcast.63, f32[128,16]{1,0:T(8,128)S(1)} %mul.706), kind=kLoop, calls=%fused_computation.25.clone.1 | loop fusion | flops 770048 | bytes 1155072 | tf_op jit(solution)/shard_map/while/body/eval_jaxpr/reduce_sum | solution.py:53
  417.0 1.7 collective-permute-start
  421.5 19.2 %fusion.44 = f32[2048,128]{1,0:T(8,128)S(1)} fusion(f32[128,16]{0,1:T(8,128)S(1)} %copy.39, f32[128]{0:T(128)S(1)} %get-tuple-element.356, f32[128]{0:T(128)S(1)} %get-tuple-element.357, f32[128]{0:T(128)S(1)} %get-tuple-element.358, f32[2048]{0:T(1024)S(1)} %bitcast.67, f32[128,16]{0,1:T(8,128)S(1)} %copy.40, f32[2048]{0:T(1024)S(1)} %broadcast_in_dim.133, ...), kind=kLoop, calls=%fused_computation.24.clone.1 | loop fusion | flops 117178368 | bytes 1132032 | tf_op jit(solution)/shard_map/while/body/eval_jaxpr/reduce_sum | solution.py:49
  440.8 3.2 reshape.484
  444.2 7.4 %multiply_reduce_fusion.3 = f32[128,4,32]{2,1,0:T(4,128)S(1)} fusion(f32[128,16,4,32]{3,2,1,0:T(4,128)} %reshape.484, f32[128,16,4]{2,1,0:T(8,128)S(1)} %bitcast.63, f32[128,16]{1,0:T(8,128)S(1)} %mul.706), kind=kLoop, calls=%fused_computation.25.clone.1 | loop fusion | flops 770048 | bytes 1155072 | tf_op jit(solution)/shard_map/while/body/eval_jaxpr/reduce_sum | solution.py:53
  455.0 19.2 %fusion.44 = f32[2048,128]{1,0:T(8,128)S(1)} fusion(f32[128,16]{0,1:T(8,128)S(1)} %copy.39, f32[128]{0:T(128)S(1)} %get-tuple-element.356, f32[128]{0:T(128)S(1)} %get-tuple-element.357, f32[128]{0:T(128)S(1)} %get-tuple-element.358, f32[2048]{0:T(1024)S(1)} %bitcast.67, f32[128,16]{0,1:T(8,128)S(1)} %copy.40, f32[2048]{0:T(1024)S(1)} %broadcast_in_dim.133, ...), kind=kLoop, calls=%fused_computation.24.clone.1 | loop fusion | flops 117178368 | bytes 1132032 | tf_op jit(solution)/shard_map/while/body/eval_jaxpr/reduce_sum | solution.py:49
  474.2 3.2 reshape.484
  477.6 7.4 %multiply_reduce_fusion.3 = f32[128,4,32]{2,1,0:T(4,128)S(1)} fusion(f32[128,16,4,32]{3,2,1,0:T(4,128)} %reshape.484, f32[128,16,4]{2,1,0:T(8,128)S(1)} %bitcast.63, f32[128,16]{1,0:T(8,128)S(1)} %mul.706), kind=kLoop, calls=%fused_computation.25.clone.1 | loop fusion | flops 770048 | bytes 1155072 | tf_op jit(solution)/shard_map/while/body/eval_jaxpr/reduce_sum | solution.py:53
  488.4 19.2 %fusion.44 = f32[2048,128]{1,0:T(8,128)S(1)} fusion(f32[128,16]{0,1:T(8,128)S(1)} %copy.39, f32[128]{0:T(128)S(1)} %get-tuple-element.356, f32[128]{0:T(128)S(1)} %get-tuple-element.357, f32[128]{0:T(128)S(1)} %get-tuple-element.358, f32[2048]{0:T(1024)S(1)} %bitcast.67, f32[128,16]{0,1:T(8,128)S(1)} %copy.40, f32[2048]{0:T(1024)S(1)} %broadcast_in_dim.133, ...), kind=kLoop, calls=%fused_computation.24.clone.1 | loop fusion | flops 117178368 | bytes 1132032 | tf_op jit(solution)/shard_map/while/body/eval_jaxpr/reduce_sum | solution.py:49
  507.6 3.2 reshape.484
  511.0 7.4 %multiply_reduce_fusion.3 = f32[128,4,32]{2,1,0:T(4,128)S(1)} fusion(f32[128,16,4,32]{3,2,1,0:T(4,128)} %reshape.484, f32[128,16,4]{2,1,0:T(8,128)S(1)} %bitcast.63, f32[128,16]{1,0:T(8,128)S(1)} %mul.706), kind=kLoop, calls=%fused_computation.25.clone.1 | loop fusion | flops 770048 | bytes 1155072 | tf_op jit(solution)/shard_map/while/body/eval_jaxpr/reduce_sum | solution.py:53
  522.1 19.2 %fusion.27 = f32[2048,128]{1,0:T(8,128)S(1)} fusion(f32[128,16]{0,1:T(8,128)S(1)} %copy.29, f32[128]{0:T(128)S(1)} %get-tuple-element.273, f32[128]{0:T(128)S(1)} %get-tuple-element.274, f32[128]{0:T(128)S(1)} %get-tuple-element.272, f32[2048]{0:T(1024)S(1)} %bitcast.71, f32[128,16]{0,1:T(8,128)S(1)} %copy.28, f32[2048]{0:T(1024)S(1)} %broadcast_in_dim.110, ...), kind=kLoop, calls=%fused_computation.57 | loop fusion | flops 117178368 | bytes 1132032 | tf_op jit(solution)/shard_map/reduce_sum | solution.py:49
  541.3 3.2 reshape.465
  544.5 7.4 %multiply_reduce_fusion.1 = f32[128,4,32]{2,1,0:T(4,128)S(1)} fusion(f32[128,16,4,32]{3,2,1,0:T(4,128)} %reshape.465, f32[128,16,4]{2,1,0:T(8,128)S(1)} %bitcast.65, f32[128,16]{1,0:T(8,128)S(1)} %reshape.464), kind=kLoop, calls=%fused_computation.58 | loop fusion | flops 770048 | bytes 1155072 | tf_op jit(solution)/shard_map/reduce_sum | solution.py:53
  552.4 2.7 reshape.469
  555.1 4.0 copy.32
  559.2 1.1 reshape.475
  560.3 1.3 copy.33
  561.6 2.6 scatter_custom_fusion
  564.2 1.6 all_to_all.8
  565.9 39.2 %all_to_all.12 = f32[128,4,1024]{2,1,0:T(4,128)S(1)} all-to-all(f32[128,4,1024]{2,1,0:T(4,128)} %all_to_all.8), channel_id=1, replica_groups=mesh['rows'=8,'blk'=16] {'rows','blk'}, dimensions={0} | all-to-all | bytes 4194304 | tf_op jit(solution)/shard_map/all_to_all | solution.py:122
  605.1 1.7 all_to_all.10
  (496 shorter events, 58.8 us)
Async XLA Ops:
  4.0 516.6 %copy-start.1 = (s32[1,256,1]{1,2,0:T(1,128)S(1)}, s32[1,256,1]{1,2,0:T(1,128)}, u32[]{:S(2)}) copy-start(s32[1,256,1]{1,2,0:T(1,128)} %param.13) | copy-start | bytes 3076
  4.0 28.3 %copy-start = (f32[2048]{0:T(1024)S(1)}, f32[2048]{0:T(1024)}, u32[]{:S(2)}) copy-start(f32[2048]{0:T(1024)} %get-tuple-element.409) | copy-start | bytes 24580 | tf_op jit(solution)/shard_map/while
  4.0 36.3 %collective-permute-start = (f32[8576]{0:T(1024)S(1)}, f32[8576]{0:T(1024)S(1)}, u32[]{:S(2)}, u32[]{:S(2)}) collective-permute-start(f32[8576]{0:T(1024)S(1)} %copy.50), channel_id=1, source_target_pairs={{15,0},{0,1},{1,2},{2,3},{3,4},{4,5},{5,6},{6,7},{7,8},{8,9},{9,10... | collective-permute-start | bytes 102920 | tf_op jit(solution)/shard_map/while/body/eval_jaxpr/ppermute | solution.py:18
  40.3 25.4 %copy-start = (f32[2048]{0:T(1024)S(1)}, f32[2048]{0:T(1024)}, u32[]{:S(2)}) copy-start(f32[2048]{0:T(1024)} %get-tuple-element.409) | copy-start | bytes 24580 | tf_op jit(solution)/shard_map/while
  40.4 33.4 %collective-permute-start = (f32[8576]{0:T(1024)S(1)}, f32[8576]{0:T(1024)S(1)}, u32[]{:S(2)}, u32[]{:S(2)}) collective-permute-start(f32[8576]{0:T(1024)S(1)} %copy.50), channel_id=1, source_target_pairs={{15,0},{0,1},{1,2},{2,3},{3,4},{4,5},{5,6},{6,7},{7,8},{8,9},{9,10... | collective-permute-start | bytes 102920 | tf_op jit(solution)/shard_map/while/body/eval_jaxpr/ppermute | solution.py:18
  73.8 27.3 %copy-start = (f32[2048]{0:T(1024)S(1)}, f32[2048]{0:T(1024)}, u32[]{:S(2)}) copy-start(f32[2048]{0:T(1024)} %get-tuple-element.409) | copy-start | bytes 24580 | tf_op jit(solution)/shard_map/while
  73.8 35.3 %collective-permute-start = (f32[8576]{0:T(1024)S(1)}, f32[8576]{0:T(1024)S(1)}, u32[]{:S(2)}, u32[]{:S(2)}) collective-permute-start(f32[8576]{0:T(1024)S(1)} %copy.50), channel_id=1, source_target_pairs={{15,0},{0,1},{1,2},{2,3},{3,4},{4,5},{5,6},{6,7},{7,8},{8,9},{9,10... | collective-permute-start | bytes 102920 | tf_op jit(solution)/shard_map/while/body/eval_jaxpr/ppermute | solution.py:18
  109.1 25.4 %copy-start = (f32[2048]{0:T(1024)S(1)}, f32[2048]{0:T(1024)}, u32[]{:S(2)}) copy-start(f32[2048]{0:T(1024)} %get-tuple-element.409) | copy-start | bytes 24580 | tf_op jit(solution)/shard_map/while
  109.1 33.4 %collective-permute-start = (f32[8576]{0:T(1024)S(1)}, f32[8576]{0:T(1024)S(1)}, u32[]{:S(2)}, u32[]{:S(2)}) collective-permute-start(f32[8576]{0:T(1024)S(1)} %copy.50), channel_id=1, source_target_pairs={{15,0},{0,1},{1,2},{2,3},{3,4},{4,5},{5,6},{6,7},{7,8},{8,9},{9,10... | collective-permute-start | bytes 102920 | tf_op jit(solution)/shard_map/while/body/eval_jaxpr/ppermute | solution.py:18
  142.5 27.0 %copy-start = (f32[2048]{0:T(1024)S(1)}, f32[2048]{0:T(1024)}, u32[]{:S(2)}) copy-start(f32[2048]{0:T(1024)} %get-tuple-element.409) | copy-start | bytes 24580 | tf_op jit(solution)/shard_map/while
  142.5 35.0 %collective-permute-start = (f32[8576]{0:T(1024)S(1)}, f32[8576]{0:T(1024)S(1)}, u32[]{:S(2)}, u32[]{:S(2)}) collective-permute-start(f32[8576]{0:T(1024)S(1)} %copy.50), channel_id=1, source_target_pairs={{15,0},{0,1},{1,2},{2,3},{3,4},{4,5},{5,6},{6,7},{7,8},{8,9},{9,10... | collective-permute-start | bytes 102920 | tf_op jit(solution)/shard_map/while/body/eval_jaxpr/ppermute | solution.py:18
  177.5 25.4 %copy-start = (f32[2048]{0:T(1024)S(1)}, f32[2048]{0:T(1024)}, u32[]{:S(2)}) copy-start(f32[2048]{0:T(1024)} %get-tuple-element.409) | copy-start | bytes 24580 | tf_op jit(solution)/shard_map/while
  177.5 33.4 %collective-permute-start = (f32[8576]{0:T(1024)S(1)}, f32[8576]{0:T(1024)S(1)}, u32[]{:S(2)}, u32[]{:S(2)}) collective-permute-start(f32[8576]{0:T(1024)S(1)} %copy.50), channel_id=1, source_target_pairs={{15,0},{0,1},{1,2},{2,3},{3,4},{4,5},{5,6},{6,7},{7,8},{8,9},{9,10... | collective-permute-start | bytes 102920 | tf_op jit(solution)/shard_map/while/body/eval_jaxpr/ppermute | solution.py:18
  210.9 27.2 %copy-start = (f32[2048]{0:T(1024)S(1)}, f32[2048]{0:T(1024)}, u32[]{:S(2)}) copy-start(f32[2048]{0:T(1024)} %get-tuple-element.409) | copy-start | bytes 24580 | tf_op jit(solution)/shard_map/while
  210.9 35.2 %collective-permute-start = (f32[8576]{0:T(1024)S(1)}, f32[8576]{0:T(1024)S(1)}, u32[]{:S(2)}, u32[]{:S(2)}) collective-permute-start(f32[8576]{0:T(1024)S(1)} %copy.50), channel_id=1, source_target_pairs={{15,0},{0,1},{1,2},{2,3},{3,4},{4,5},{5,6},{6,7},{7,8},{8,9},{9,10... | collective-permute-start | bytes 102920 | tf_op jit(solution)/shard_map/while/body/eval_jaxpr/ppermute | solution.py:18
  246.1 25.4 %copy-start = (f32[2048]{0:T(1024)S(1)}, f32[2048]{0:T(1024)}, u32[]{:S(2)}) copy-start(f32[2048]{0:T(1024)} %get-tuple-element.409) | copy-start | bytes 24580 | tf_op jit(solution)/shard_map/while
  246.1 33.4 %collective-permute-start = (f32[8576]{0:T(1024)S(1)}, f32[8576]{0:T(1024)S(1)}, u32[]{:S(2)}, u32[]{:S(2)}) collective-permute-start(f32[8576]{0:T(1024)S(1)} %copy.50), channel_id=1, source_target_pairs={{15,0},{0,1},{1,2},{2,3},{3,4},{4,5},{5,6},{6,7},{7,8},{8,9},{9,10... | collective-permute-start | bytes 102920 | tf_op jit(solution)/shard_map/while/body/eval_jaxpr/ppermute | solution.py:18
  279.5 27.3 %copy-start = (f32[2048]{0:T(1024)S(1)}, f32[2048]{0:T(1024)}, u32[]{:S(2)}) copy-start(f32[2048]{0:T(1024)} %get-tuple-element.409) | copy-start | bytes 24580 | tf_op jit(solution)/shard_map/while
  279.5 35.3 %collective-permute-start = (f32[8576]{0:T(1024)S(1)}, f32[8576]{0:T(1024)S(1)}, u32[]{:S(2)}, u32[]{:S(2)}) collective-permute-start(f32[8576]{0:T(1024)S(1)} %copy.50), channel_id=1, source_target_pairs={{15,0},{0,1},{1,2},{2,3},{3,4},{4,5},{5,6},{6,7},{7,8},{8,9},{9,10... | collective-permute-start | bytes 102920 | tf_op jit(solution)/shard_map/while/body/eval_jaxpr/ppermute | solution.py:18
  314.8 25.4 %copy-start = (f32[2048]{0:T(1024)S(1)}, f32[2048]{0:T(1024)}, u32[]{:S(2)}) copy-start(f32[2048]{0:T(1024)} %get-tuple-element.409) | copy-start | bytes 24580 | tf_op jit(solution)/shard_map/while
  314.8 33.4 %collective-permute-start = (f32[8576]{0:T(1024)S(1)}, f32[8576]{0:T(1024)S(1)}, u32[]{:S(2)}, u32[]{:S(2)}) collective-permute-start(f32[8576]{0:T(1024)S(1)} %copy.50), channel_id=1, source_target_pairs={{15,0},{0,1},{1,2},{2,3},{3,4},{4,5},{5,6},{6,7},{7,8},{8,9},{9,10... | collective-permute-start | bytes 102920 | tf_op jit(solution)/shard_map/while/body/eval_jaxpr/ppermute | solution.py:18
  348.2 27.3 %copy-start = (f32[2048]{0:T(1024)S(1)}, f32[2048]{0:T(1024)}, u32[]{:S(2)}) copy-start(f32[2048]{0:T(1024)} %get-tuple-element.409) | copy-start | bytes 24580 | tf_op jit(solution)/shard_map/while
  348.3 35.3 %collective-permute-start = (f32[8576]{0:T(1024)S(1)}, f32[8576]{0:T(1024)S(1)}, u32[]{:S(2)}, u32[]{:S(2)}) collective-permute-start(f32[8576]{0:T(1024)S(1)} %copy.50), channel_id=1, source_target_pairs={{15,0},{0,1},{1,2},{2,3},{3,4},{4,5},{5,6},{6,7},{7,8},{8,9},{9,10... | collective-permute-start | bytes 102920 | tf_op jit(solution)/shard_map/while/body/eval_jaxpr/ppermute | solution.py:18
  383.5 25.4 %copy-start = (f32[2048]{0:T(1024)S(1)}, f32[2048]{0:T(1024)}, u32[]{:S(2)}) copy-start(f32[2048]{0:T(1024)} %get-tuple-element.409) | copy-start | bytes 24580 | tf_op jit(solution)/shard_map/while
  383.6 33.4 %collective-permute-start = (f32[8576]{0:T(1024)S(1)}, f32[8576]{0:T(1024)S(1)}, u32[]{:S(2)}, u32[]{:S(2)}) collective-permute-start(f32[8576]{0:T(1024)S(1)} %copy.50), channel_id=1, source_target_pairs={{15,0},{0,1},{1,2},{2,3},{3,4},{4,5},{5,6},{6,7},{7,8},{8,9},{9,10... | collective-permute-start | bytes 102920 | tf_op jit(solution)/shard_map/while/body/eval_jaxpr/ppermute | solution.py:18
  416.9 27.0 %copy-start = (f32[2048]{0:T(1024)S(1)}, f32[2048]{0:T(1024)}, u32[]{:S(2)}) copy-start(f32[2048]{0:T(1024)} %get-tuple-element.409) | copy-start | bytes 24580 | tf_op jit(solution)/shard_map/while
  417.0 35.0 %collective-permute-start = (f32[8576]{0:T(1024)S(1)}, f32[8576]{0:T(1024)S(1)}, u32[]{:S(2)}, u32[]{:S(2)}) collective-permute-start(f32[8576]{0:T(1024)S(1)} %copy.50), channel_id=1, source_target_pairs={{15,0},{0,1},{1,2},{2,3},{3,4},{4,5},{5,6},{6,7},{7,8},{8,9},{9,10... | collective-permute-start | bytes 102920 | tf_op jit(solution)/shard_map/while/body/eval_jaxpr/ppermute | solution.py:18
  452.0 25.4 %copy-start = (f32[2048]{0:T(1024)S(1)}, f32[2048]{0:T(1024)}, u32[]{:S(2)}) copy-start(f32[2048]{0:T(1024)} %get-tuple-element.409) | copy-start | bytes 24580 | tf_op jit(solution)/shard_map/while
  452.0 33.4 %collective-permute-start = (f32[8576]{0:T(1024)S(1)}, f32[8576]{0:T(1024)S(1)}, u32[]{:S(2)}, u32[]{:S(2)}) collective-permute-start(f32[8576]{0:T(1024)S(1)} %copy.50), channel_id=1, source_target_pairs={{15,0},{0,1},{1,2},{2,3},{3,4},{4,5},{5,6},{6,7},{7,8},{8,9},{9,10... | collective-permute-start | bytes 102920 | tf_op jit(solution)/shard_map/while/body/eval_jaxpr/ppermute | solution.py:18
  485.4 25.4 %copy-start = (f32[2048]{0:T(1024)S(1)}, f32[2048]{0:T(1024)}, u32[]{:S(2)}) copy-start(f32[2048]{0:T(1024)} %get-tuple-element.409) | copy-start | bytes 24580 | tf_op jit(solution)/shard_map/while
  485.4 33.4 %collective-permute-start = (f32[8576]{0:T(1024)S(1)}, f32[8576]{0:T(1024)S(1)}, u32[]{:S(2)}, u32[]{:S(2)}) collective-permute-start(f32[8576]{0:T(1024)S(1)} %copy.50), channel_id=1, source_target_pairs={{15,0},{0,1},{1,2},{2,3},{3,4},{4,5},{5,6},{6,7},{7,8},{8,9},{9,10... | collective-permute-start | bytes 102920 | tf_op jit(solution)/shard_map/while/body/eval_jaxpr/ppermute | solution.py:18
where the time goes:
time: 611 us; the launch traced here: 607 us
  other arithmetic  428 us (70%)
  local copies, waits for them, and re-layouts  121 us (20%)
  blocking collectives  39.2 us (6%)
  starting transfers between devices  15.7 us (3%)
    reduce_sum x16, other arithmetic, row_block(): jnp.sum(kernel.reshape(rows * Q, patches, Q), axis=2)  307 us
    reduce_sum x16, other arithmetic, row_block(): folded = jnp.sum(summed * quad_weights[:, :, None] * active, axis=1)  119 us
    reshape x16, local copies, waits for them, and re-layouts, row_block(): jnp.sum(kernel.reshape(rows * Q, patches, Q), axis=2)  50.6 us
    all_to_all x1, blocking collectives, on_device(): lax.all_to_all(outgoing, ('rows', 'blk'), split_axis=0, concat_axis=0, ti...  39.2 us
    ppermute x15, starting transfers between devices, passed_along(): return lax.ppermute(block, axis, route)  15.7 us
    slice x32, local copies, waits for them, and re-layouts, row_block(): delta_x = col_points[0][None, :] - row_points[0][:, None]  14.7 us
    slice x16, local copies, waits for them, and re-layouts, row_block(): row_vecs[0][:, None] * delta_x + row_vecs[1][:, None] * delta_y  13.1 us
  transfers between devices with their start and end apart: 15, of which 0 were waited for; matrix products, arithmetic and copies ran while one was open for 82% of the time, Pallas kernels for 0%

commit v1 on v0

v1 whole, which is shorter than its diff:
```python
import functools
import math

import jax
import jax.numpy as jnp
from jax import lax
from jax.experimental import pallas as pl
from jax.experimental.pallas import tpu as pltpu
from jax.sharding import PartitionSpec as P

Q = 16
TS = 32
GROUP = 4
softening = 0.05
BF = jnp.bfloat16
F32 = jnp.float32


def three_parts(x):
    high = x.astype(BF)
    rest = x - high.astype(F32)
    middle = rest.astype(BF)
    low = (rest - middle.astype(F32)).astype(BF)
    return high, middle, low


def features_kernel(cols_ref, norm_ref, out_ref):
    row = lax.broadcasted_iota(jnp.int32, (8, TS * Q), 0)
    for tile in range(cols_ref.shape[1]):
        cols = cols_ref[0, tile]
        x, y, z, w = (cols[f : f + 1] for f in range(4))
        normal = norm_ref[0, tile]
        nx, ny, nz = (jnp.concatenate([normal[f : f + 1]] * 4, axis=1) for f in range(3))
        square = x * x + y * y + z * z
        depth = nx * x + ny * y + nz * z
        scale = w * (1.0 / math.pi)
        pick = lambda *rows: functools.reduce(
            lambda acc, at: jnp.where(row == at, rows[at], acc), range(len(rows)), jnp.zeros((8, TS * Q), F32)
        )
        ours = pick(x, y, z, square, jnp.ones_like(x))
        half = scale * -0.5
        theirs = pick(nx * half, ny * half, nz * half, -depth * scale)
        both = jnp.concatenate([ours, theirs], axis=1)
        high = both.astype(BF).astype(F32)
        rest = both - high
        middle = rest.astype(BF).astype(F32)
        low = rest - middle
        out_ref[tile] = jnp.concatenate([high, high, high, middle, middle, low], axis=0).astype(BF)


def features(cols, normals):
    sources, span = cols.shape[:2]
    width = TS * Q
    return pl.pallas_call(
        features_kernel,
        grid=(sources,),
        in_specs=[
            pl.BlockSpec((1, span, 4, width), lambda s: (s, 0, 0, 0)),
            pl.BlockSpec((1, span, 3, 128), lambda s: (s, 0, 0, 0)),
        ],
        out_specs=pl.BlockSpec((span, 48, 2 * width), lambda s: (s, 0, 0)),
        out_shape=jax.ShapeDtypeStruct((sources * span, 48, 2 * width), BF),
        compiler_params=pltpu.CompilerParams(vmem_limit_bytes=40 * 2**20),
    )(cols, normals)


def tiles_kernel(total_ref, groups_ref, units_ref, lhs_ref, rhs_ref, out_ref):
    out_ref[...] = jnp.zeros_like(out_ref)
    lane = lax.broadcasted_iota(jnp.int32, (8, 128), 1)
    odd = (lane // TS) % 2 == 1
    upper = lane // (2 * TS) == 1
    width = TS * Q
    last = groups_ref.shape[0] - 1

    def one_group(_, carry):
        tile, at = carry
        codes = [units_ref[tile * 64 + at * GROUP + g] for g in range(GROUP)]
        rows = [code % 128 for code in codes]
        gap = jnp.concatenate([lhs_ref[r, :TS] for r in rows], axis=0)
        facing = jnp.concatenate([lhs_ref[r, TS:] for r in rows], axis=0)
        sums = [None] * (GROUP * 4)
        for part in range(width // 256):
            ours = rhs_ref[tile, :, part * 256 : (part + 1) * 256]
            theirs = rhs_ref[tile, :, width + part * 256 : width + (part + 1) * 256]
            spread = jnp.dot(gap, ours, preferred_element_type=F32)
            cos_row = jnp.dot(facing, ours, preferred_element_type=F32)
            cos_col = jnp.dot(gap, theirs, preferred_element_type=F32)
            value = (
                jnp.maximum(cos_row, 0.0)
                * jnp.maximum(cos_col, 0.0)
                * pl.reciprocal(spread * spread, approx=True)
            )
            for v in range(GROUP * 4):
                piece = value[v * 8 : v * 8 + 8]
                piece = piece[:, :128] + piece[:, 128:]
                sums[v] = piece if sums[v] is None else sums[v] + piece
        for g in range(GROUP):
            a0, a1, a2, a3 = sums[g * 4 : g * 4 + 4]
            low = jnp.where(odd, a1, a0) + pltpu.roll(jnp.where(odd, a0, a1), TS, 1)
            high = jnp.where(odd, a3, a2) + pltpu.roll(jnp.where(odd, a2, a3), TS, 1)
            mixed = jnp.where(upper, high, low) + pltpu.roll(jnp.where(upper, low, high), 2 * TS, 1)
            slot = codes[g] // 128
            out_ref[slot] = out_ref[slot] + mixed
        done = at + 1 >= groups_ref[tile]
        return (jnp.where(done, jnp.minimum(tile + 1, last), tile), jnp.where(done, 0, at + 1))

    lax.fori_loop(0, total_ref[0], one_group, (jnp.int32(0), jnp.int32(0)))


def assemble(total, groups, units, lhs, rhs, slots):
    smem = pl.BlockSpec(memory_space=pltpu.SMEM)
    vmem = pl.BlockSpec(memory_space=pltpu.VMEM)
    return pl.pallas_call(
        tiles_kernel,
        in_specs=[smem, smem, smem, vmem, vmem],
        out_specs=vmem,
        out_shape=jax.ShapeDtypeStruct((slots, 8, 128), F32),
        compiler_params=pltpu.CompilerParams(vmem_limit_bytes=56 * 2**20),
    )(total, groups, units, lhs, rhs)


def rounded(x):
    return lax.reduce_precision(x, 8, 7)


def row_features(points, normals, weights):
    span = normals.shape[1] // TS
    area = jnp.sum(weights.reshape(-1, Q), axis=1, keepdims=True)
    scale = (area / weights.reshape(-1, Q)).reshape(-1)
    x, y, z = points
    nx, ny, nz = jnp.repeat(normals, Q, axis=1)
    square = x * x + y * y + z * z + softening
    depth = nx * x + ny * y + nz * z
    zero = jnp.zeros_like(x)
    gap = [-2.0 * x * scale, -2.0 * y * scale, -2.0 * z * scale, scale, square * scale, zero, zero, zero]
    facing = [nx, ny, nz, zero, -depth, zero, zero, zero]
    rows = jnp.stack([jnp.stack(gap), jnp.stack(facing)])
    rows = rows.reshape(2, 8, span, 8, 4, Q).transpose(2, 5, 0, 4, 3, 1)
    rows = rows.reshape(span * Q, 2 * TS, 8)
    pad = jnp.zeros((1, 2 * TS, 8), F32).at[0, :TS, 4].set(1.0)
    rows = jnp.concatenate([rows, pad])
    high = rounded(rows)
    middle = rounded(rows - high)
    low = rounded(rows - high - middle)
    return jnp.concatenate([high, middle, low, high, middle, high], axis=2).astype(BF)


def work_list(visible, quad_mask, targets, capacity):
    span, columns = visible.shape
    order = jnp.arange(targets.shape[0], dtype=jnp.int32)
    same = targets[:, None] == targets[None, :]
    rank = jnp.sum((same & (order[:, None] > order[None, :])).astype(jnp.int32), axis=1)
    slot = (targets * capacity + rank).reshape(span, columns)
    shifts = jnp.arange(Q, dtype=jnp.int32)
    used = ((quad_mask[:, None, :] >> shifts[None, :, None]) & 1) * visible[:, None, :]
    pair = jnp.arange(span * Q, dtype=jnp.int32)
    code = (slot[:, None, :] * 128 + pair.reshape(span, Q)[:, :, None]).reshape(span * Q, columns)
    used = used.reshape(span * Q, columns)
    place = jnp.sum(jnp.where(pair[:, None] > pair[None, :], 1, 0)[:, :, None] * used[None], axis=1)
    count = jnp.sum(used, axis=0)
    idle = span * Q
    hit = (place[:, None, :] == pair[None, :, None]) & (used[:, None, :] > 0)
    units = jnp.sum(jnp.where(hit, code[:, None, :] - idle, 0), axis=0) + idle
    groups = jnp.maximum((count + GROUP - 1) // GROUP, 1)
    return jnp.sum(groups)[None], groups, units.T.reshape(-1)


def on_device(points, normals, weights, visible, quad_mask, owners):
    devices = lax.axis_size("rows") * lax.axis_size("blk")
    sources = lax.axis_size("blk")
    span = normals.shape[1] // TS
    capacity = max(2, 2 * owners.shape[1] // devices)
    flat = jnp.concatenate([points, weights[None]])
    cols = flat.reshape(4, span, TS, Q).transpose(1, 0, 3, 2).reshape(-1, 128)
    tiled = jnp.tile(normals.reshape(3, span, 1, TS).transpose(1, 0, 2, 3), (1, 1, 4, 1)).reshape(-1, 128)
    packed = jnp.concatenate([cols, tiled, jnp.zeros((-(cols.shape[0] + tiled.shape[0]) % 8, 128), F32)])
    spread = jnp.broadcast_to(packed[None], (sources,) + packed.shape)
    gathered = lax.all_to_all(spread, "blk", split_axis=0, concat_axis=0, tiled=True)
    all_cols = gathered[:, : cols.shape[0]].reshape(sources, span, 4, TS * Q)
    all_normals = gathered[:, cols.shape[0] : cols.shape[0] + tiled.shape[0]].reshape(sources, span, 3, 128)
    rhs = features(all_cols, all_normals)
    lhs = row_features(points, normals, weights)
    total, groups, units = work_list(visible, quad_mask, owners[0, :, 0], capacity)
    out = assemble(total, groups, units, lhs, rhs, devices * capacity)
    arrived = lax.all_to_all(
        out.reshape(devices, capacity * 8, 128), ("rows", "blk"), split_axis=0, concat_axis=0, tiled=True
    )
    return arrived.reshape(devices * capacity, TS * TS)


def solution(mesh):
    placed = (
        P(None, ("rows", "blk")),
        P(None, ("rows", "blk")),
        P(("rows", "blk")),
        P(("rows", "blk"), None),
        P(("rows", "blk"), None),
        P(("rows", "blk"), None, None),
    )
    return jax.shard_map(
        on_device, mesh=mesh, in_specs=placed, out_specs=P(("rows", "blk"), None), check_vma=False
    )
```

time: 611 us -> 260 us (0.43)
  other arithmetic: 428 us -> 6.84 us
  Pallas kernels: 0 us -> 163 us
  local copies, waits for them, and re-layouts: 121 us -> 26.7 us
  blocking collectives: 39.2 us -> 52.5 us
  starting transfers between devices: 15.7 us -> 9.46 us
    reduce_sum x34 -> x6, other arithmetic: 426 us -> 3.01 us  [the longest x1 1.25 us: work_list(): return (jnp.sum(groups)[None], groups, units.T.reshape(-1))]
    pallas_call x0 -> x2, Pallas kernels: none -> 163 us  [the longest x1 161 us: assemble(): pl.pallas_call(tiles_kernel, in_specs=[smem, smem, smem, vmem, vmem], out...]
    reshape x37 -> x8, local copies, waits for them, and re-layouts: 58.6 us -> 3.84 us  [the longest x1 1.48 us: on_device(): return arrived.reshape(devices * capacity, TS * TS)]
    slice x64 -> x2, local copies, waits for them, and re-layouts: 27.9 us -> 2 us  [the longest x1 1.08 us: on_device(): all_cols = gathered[:, :cols.shape[0]].reshape(sources, span, 4, TS * Q)]
    ppermute x15 -> x0, starting transfers between devices: 15.7 us -> none  [passed_along(): return lax.ppermute(block, axis, route)]
    all_to_all x1, blocking collectives: 39.2 us -> 52.5 us  [on_device(): lax.all_to_all(out.reshape(devices, capacity * 8, 128), ('rows', 'blk'),...]
    all_to_all x0 -> x1, starting transfers between devices: none -> 9.46 us  [on_device(): lax.all_to_all(spread, 'blk', split_axis=0, concat_axis=0, tiled=True)]
    concatenate x0 -> x5, local copies, waits for them, and re-layouts: none -> 9.06 us  [the longest x1 4.4 us: row_features(): jnp.concatenate([high, middle, low, high, middle, high], axis=2).astype(BF)]
  transfers between devices with their start and end apart: 15 -> 1, of which waited for: 0 -> 0; matrix products, arithmetic and copies ran while one was open for 82% -> 9% of each run, Pallas kernels for 0% -> 0%
where the time goes in v1:
time: 260 us; the launch traced here: 259 us
  Pallas kernels  163 us (63%)
  blocking collectives  52.5 us (20%)
  local copies, waits for them, and re-layouts  26.7 us (10%)
  starting transfers between devices  9.46 us (4%)
  other arithmetic  6.84 us (3%)
    pallas_call x1, Pallas kernels, assemble(): pl.pallas_call(tiles_kernel, in_specs=[smem, smem, smem, vmem, vmem], out...  161 us
    all_to_all x1, blocking collectives, on_device(): lax.all_to_all(out.reshape(devices, capacity * 8, 128), ('rows', 'blk'),...  52.5 us
    all_to_all x1, starting transfers between devices, on_device(): lax.all_to_all(spread, 'blk', split_axis=0, concat_axis=0, tiled=True)  9.46 us
  transfers between devices with their start and end apart: 1, of which 0 were waited for; matrix products, arithmetic and copies ran while one was open for 9% of the time, Pallas kernels for 0%

profile of v1, /device:TPU:1, one launch (start us, length us, event | category | flops | bytes accessed | tf_op | source)
XLA Modules:
  0.0 259.1 jit_solution(6555982286767571146)
XLA Ops:
  0.0 0.8 reshape.289
  0.9 0.1 tile.12
  0.9 0.8 concatenate.27
  1.7 0.9 concatenate.26
  2.6 0.1 copy.71
  2.8 0.1 reshape.288
  2.9 0.1 pad.5.clone
  3.0 0.1 maximum_maximum_fusion
  3.0 0.9 broadcast_in_dim.89
  3.9 9.5 %all-to-all-start = ((f32[16,80,128]{2,1,0:T(8,128)}), f32[16,80,128]{2,1,0:T(8,128)}, u32[]{:S(2)}, u32[]{:S(2)}) async-start(f32[16,80,128]{2,1,0:T(8,128)} %broadcast_in_dim.89), calls=%async_computation | async-start | bytes 1310720 | tf_op jit(solution)/shard_map/all_to_all | solution.py:178
  13.4 0.1 shift_right_arithmetic.43
  13.5 0.1 broadcast_compare_fusion
  13.6 0.1 bitcast_multiply_fusion
  13.7 0.1 reshape.286
  13.8 0.2 convert_reduce_fusion
  14.0 0.1 reduce_sum.60
  14.1 0.1 mul.124
  14.1 0.1 broadcast_in_dim_reshape.15
  14.2 0.1 broadcast_in_dim.76
  14.3 0.1 copy.62
  14.5 0.1 broadcast_in_dim.78
  14.6 0.1 copy.63
  14.7 0.1 broadcast_in_dim.80
  14.8 0.1 copy.64
  15.0 0.1 broadcast_in_dim.82
  15.0 0.1 broadcast_in_dim.83
  15.2 0.1 fusion.4
  15.3 0.8 multiply_reduce_fusion
  16.0 0.7 select_reduce_fusion
  16.7 0.1 copy.56
  16.8 0.7 reshape.285.units_ref
  17.6 0.1 broadcast_in_dim.87
  17.7 0.1 broadcast_in_dim.84
  17.7 0.1 broadcast_in_dim.85
  17.9 0.1 stack.40
  18.0 0.1 reduce_sum.62
  18.1 0.1 div.29
  18.2 0.1 div.30
  18.3 0.1 stack.35
  18.4 0.1 stack.34
  18.6 0.1 stack.36
  18.7 0.1 stack.33
  18.8 0.1 stack.32
  19.2 0.1 broadcast_dynamic-update-slice_fusion.4
  19.3 0.1 broadcast_dynamic-update-slice_fusion.3
  19.4 0.1 broadcast_dynamic-update-slice_fusion.2
  19.7 0.1 broadcast_dynamic-update-slice_fusion
  19.8 0.4 maximum_bitcast_fusion
  20.1 0.5 reshape.287
  20.6 0.1 fusion.8
  20.8 1.8 copy.68
  22.6 2.9 %copy.67 = f32[65,64,8]{2,1,0:T(8,128)} copy(f32[65,64,8]{0,2,1:T(8,128)S(1)} %get-tuple-element.26) | data formatting | bytes 266240 | tf_op jit(solution)/shard_map/reduce_precision | solution.py:123
  25.5 2.9 %copy.66 = f32[65,64,8]{2,1,0:T(8,128)} copy(f32[65,64,8]{0,2,1:T(8,128)S(1)} %get-tuple-element.28) | data formatting | bytes 266240 | tf_op jit(solution)/shard_map/concatenate | solution.py:141
  28.4 2.9 %fusion.1 = (bf16[65,64,8]{2,1,0:T(8,128)(2,1)S(1)}, bf16[65,64,8]{2,1,0:T(8,128)(2,1)S(1)}) fusion(f32[65,64,8]{2,1,0:T(8,128)} %copy.66, f32[65,64,8]{2,1,0:T(8,128)} %copy.67), kind=kLoop, calls=%fused_computation.3 | loop fusion | flops 199680 | bytes 399360 | tf_op jit(solution)/shard_map/convert.2
  31.3 4.4 %concatenate.25.lhs_ref = bf16[65,64,48]{2,1,0:T(8,128)(2,1)} concatenate(bf16[65,64,8]{2,1,0:T(8,128)(2,1)S(1)} %copy.68, bf16[65,64,8]{2,1,0:T(8,128)(2,1)S(1)} %get-tuple-element.25, bf16[65,64,8]{2,1,0:T(8,128)(2,1)S(1)} %get-tuple-element.24, bf16[65,64,8]{2,1,0:T(8,128)(2,1)S(1)} %copy.68, bf16[65,64,8]{2,1,0:T(8,128)(2,1)S(1)} %get-tuple-element.25, ...), dimensions={2} | concatenate | bytes 798720 | tf_op jit(solution)/shard_map/concatenate | solution.py:145
  35.7 1.2 fusion.10
  37.0 0.9 slice.39
  37.9 1.1 slice.38
  39.0 0.2 reshape.290.cols_ref
  39.3 1.8 shard_map.64.rhs_ref
  41.1 2.7 %copy-done = bf16[64,48,1024]{2,1,0:T(8,128)(2,1)} copy-done((bf16[64,48,1024]{2,1,0:T(8,128)(2,1)}, bf16[64,48,1024]{2,1,0:T(8,128)(2,1)S(1)}, u32[]{:S(2)}) %copy-start) | copy-done | bytes 6291480
  43.8 161.4 %shard_map.65 = f32[512,8,128]{2,1,0:T(8,128)} custom-call(s32[1]{0:T(128)} %bitcast.total_ref, s32[64]{0:T(128)} %get-tuple-element.23.groups_ref, s32[4096]{0:T(1024)} %reshape.285.units_ref, bf16[65,64,48]{2,1,0:T(8,128)(2,1)} %concatenate.25.lhs_ref, bf16[64,48,1024]{2,1,0:T(8,128)(2,1)} %copy-done), custom_call_target="tpu_custom_call" | custom-call | tf_op jit(solution)/shard_map/pallas_call | solution.py:113
  205.2 52.5 %all_to_all.10 = f32[128,32,128]{2,1,0:T(8,128)S(1)} all-to-all(f32[128,32,128]{2,1,0:T(8,128)} %bitcast.45), channel_id=1, replica_groups=mesh['rows'=8,'blk'=16] {'rows','blk'}, dimensions={0} | all-to-all | bytes 4194304 | tf_op jit(solution)/shard_map/all_to_all | solution.py:185
  257.7 1.5 reshape.293
  (43 shorter events, 0.8 us)
Async XLA Ops:
  0.0 13.4 %copy-start.7 = (f32[3,128]{1,0:T(4,128)S(1)}, f32[3,128]{1,0:T(4,128)}, u32[]{:S(2)}) copy-start(f32[3,128]{1,0:T(4,128)} %param.9) | copy-start | bytes 4612
  0.0 13.7 %copy-start.3 = (f32[2048]{0:T(1024)S(1)}, f32[2048]{0:T(1024)}, u32[]{:S(2)}) copy-start(f32[2048]{0:T(1024)} %param.10) | copy-start | bytes 24580
  0.0 13.5 %copy-start.5 = (s32[4,64]{1,0:T(4,128)S(1)}, s32[4,64]{1,0:T(4,128)}, u32[]{:S(2)}) copy-start(s32[4,64]{1,0:T(4,128)} %param.12) | copy-start | bytes 3076
  0.0 13.5 %copy-start.4 = (s32[4,64]{1,0:T(4,128)S(1)}, s32[4,64]{1,0:T(4,128)}, u32[]{:S(2)}) copy-start(s32[4,64]{1,0:T(4,128)} %param.11) | copy-start | bytes 3076
  0.0 13.8 %copy-start.6 = (s32[1,256,1]{1,2,0:T(1,128)S(1)}, s32[1,256,1]{1,2,0:T(1,128)}, u32[]{:S(2)}) copy-start(s32[1,256,1]{1,2,0:T(1,128)} %param.13) | copy-start | bytes 3076
  2.6 15.2 %copy-start.2 = (f32[3,2048]{1,0:T(4,128)S(1)}, f32[3,2048]{1,0:T(4,128)}, u32[]{:S(2)}) copy-start(f32[3,2048]{1,0:T(4,128)} %param.8) | copy-start | bytes 73732
  3.9 33.0 %all-to-all-start = ((f32[16,80,128]{2,1,0:T(8,128)}), f32[16,80,128]{2,1,0:T(8,128)}, u32[]{:S(2)}, u32[]{:S(2)}) async-start(f32[16,80,128]{2,1,0:T(8,128)} %broadcast_in_dim.89), calls=%async_computation | async-start | bytes 1310720 | tf_op jit(solution)/shard_map/all_to_all | solution.py:178
  19.2 1.4 copy-start.1
  41.1 2.7 %copy-start = (bf16[64,48,1024]{2,1,0:T(8,128)(2,1)}, bf16[64,48,1024]{2,1,0:T(8,128)(2,1)S(1)}, u32[]{:S(2)}) copy-start(bf16[64,48,1024]{2,1,0:T(8,128)(2,1)S(1)} %shard_map.64.rhs_ref) | copy-start | bytes 18874372

commit v2 on v1

v2 whole, which is shorter than its diff:
```python
import functools
import math

import jax
import jax.numpy as jnp
from jax import lax
from jax.experimental import pallas as pl
from jax.experimental.pallas import tpu as pltpu
from jax.sharding import PartitionSpec as P

Q = 16
TS = 32
GROUP = 4
FOLD = 16
softening = 0.05
BF = jnp.bfloat16
F32 = jnp.float32


def split(x):
    high = x.astype(BF).astype(F32)
    rest = x - high
    middle = rest.astype(BF).astype(F32)
    return high, middle, rest - middle


def by_rows(shape, values, axis=0):
    at = lax.broadcasted_iota(jnp.int32, shape, axis)
    return functools.reduce(
        lambda acc, k: jnp.where(at == k, values[k], acc), range(len(values)), jnp.zeros(shape, F32)
    )


def exact_dot(parts, selector, contract=((1,), (0,))):
    dots = [lax.dot_general(part.astype(BF), selector, (contract, ((), ())), preferred_element_type=F32) for part in parts]
    return dots[0] + dots[1] + dots[2]


def rows_kernel(points_ref, weights_ref, normals_ref, gap_ref, depth_ref, face_ref):
    width = TS * Q
    span = normals_ref.shape[1] // TS
    iota = lambda shape, axis: lax.broadcasted_iota(jnp.int32, shape, axis)
    as_ones = lambda hit: jnp.where(hit, 1.0, 0.0).astype(BF)
    row = iota((width, 1), 0)
    order = as_ones(iota((width, width), 1) == (row % 8) * 64 + (row // 8 % 4) * Q + row // TS)
    same = as_ones(iota((width, width), 1) // Q == iota((width, width), 0) // Q)
    widen = as_ones(iota((TS, width), 1) // Q == iota((TS, width), 0))
    small = iota((TS, 1), 0)
    shuffle = as_ones(iota((TS, TS), 1) == (small % 8) * 4 + small // 8)
    across = ((1,), (1,))
    for top in range(span):
        at = slice(top * width, (top + 1) * width)
        x, y, z = (points_ref[k : k + 1, at] for k in range(3))
        weight = weights_ref[:, at]
        normal = normals_ref[:, top * TS : (top + 1) * TS]
        normal = jnp.concatenate([normal, jnp.zeros((5, TS), F32)], axis=0)
        high, middle, low = split(normal)
        face = jnp.concatenate([high, middle, low, high, middle, high], axis=0).astype(BF)
        face = lax.dot_general(shuffle, face, (across, ((), ())), preferred_element_type=F32)
        face_ref[top * TS : (top + 1) * TS] = face.astype(BF)
        wide = exact_dot((high, middle, low), widen)
        depth = wide[0:1] * x + wide[1:2] * y + wide[2:3] * z
        area = exact_dot(split(jnp.broadcast_to(weight, (8, width))), same)[0:1]
        scale = area / weight
        square = x * x + y * y + z * z + softening
        gap = by_rows((8, width), [-2.0 * x * scale, -2.0 * y * scale, -2.0 * z * scale, scale, square * scale])
        high, middle, low = split(gap)
        gap = jnp.concatenate([high, middle, low, high, middle, high], axis=0).astype(BF)
        gap = lax.dot_general(order, gap, (across, ((), ())), preferred_element_type=F32)
        gap_ref[top * Q : (top + 1) * Q] = gap.astype(BF).reshape(Q, TS, 48)
        parts = [jnp.broadcast_to(part, (128, width)).astype(BF) for part in split(depth)]
        deep = [lax.dot_general(order, part, (across, ((), ())), preferred_element_type=F32) for part in parts]
        depth_ref[top * Q : (top + 1) * Q] = (deep[0] + deep[1] + deep[2]).reshape(Q, TS, 128)
    gap_ref[span * Q] = jnp.where(iota((TS, 48), 1) == 4, 1.0, 0.0).astype(BF)
    depth_ref[span * Q] = jnp.zeros((TS, 128), F32)


def row_features(points, weights, normals):
    vmem = pl.BlockSpec(memory_space=pltpu.VMEM)
    pairs = normals.shape[1] // TS * Q + 1
    return pl.pallas_call(
        rows_kernel,
        in_specs=[vmem] * 3,
        out_specs=[vmem] * 3,
        out_shape=[
            jax.ShapeDtypeStruct((pairs, TS, 48), BF),
            jax.ShapeDtypeStruct((pairs, TS, 128), F32),
            jax.ShapeDtypeStruct((normals.shape[1], 48), BF),
        ],
        compiler_params=pltpu.CompilerParams(vmem_limit_bytes=40 * 2**20),
    )(points, weights, normals)


def column_features(packed_ref, rhs_ref, source):
    width = TS * Q
    span = rhs_ref.shape[0] // packed_ref.shape[0]
    for tile in range(span):
        base = span * Q + tile * 3
        nx, ny, nz = (packed_ref[source, base + k : base + k + 1] for k in range(3))
        for lanes in range(width // 128):
            at = tile * Q + lanes * 4
            x, y, z, w = (packed_ref[source, at + k : at + k + 1] for k in range(4))
            square = x * x + y * y + z * z
            depth = nx * x + ny * y + nz * z
            scale = w * (1.0 / math.pi)
            half = scale * -0.5
            ours = by_rows((8, 128), [x, y, z, square, jnp.ones_like(x)])
            theirs = by_rows((8, 128), [nx * half, ny * half, nz * half, -depth * scale])
            for block, start in ((ours, lanes * 128), (theirs, width + lanes * 128)):
                high, middle, low = split(block)
                rhs_ref[source * span + tile, :, start : start + 128] = jnp.concatenate(
                    [high, high, high, middle, middle, low], axis=0
                ).astype(BF)


def tiles_kernel(total_ref, groups_ref, units_ref, slot_ref, lhs_ref, depth_ref, face_ref, packed_ref, out_ref, acc, near, rhs_ref):
    out_ref[...] = jnp.zeros_like(out_ref)
    acc[...] = jnp.zeros_like(acc)
    width = TS * Q
    last = rhs_ref.shape[0] - 1

    def codes_of(place):
        tile, at = place
        return [units_ref[tile * 64 + at * GROUP + g] for g in range(GROUP)]

    def following(place):
        tile, at = place
        done = at + 1 >= groups_ref[tile]
        return (jnp.where(done, tile + 1, tile), jnp.where(done, 0, at + 1))

    def work_on(place):
        codes = codes_of(place)
        rows = [code % 128 for code in codes]
        tile = jnp.minimum(place[0], last)
        gap = jnp.concatenate([lhs_ref[r] for r in rows], axis=0)
        tops = [pl.ds(pl.multiple_of(jnp.minimum(r // Q, 3) * TS, TS), TS) for r in rows]
        total = [None] * GROUP
        for part in range(width // 256):
            at = slice(part * 256, (part + 1) * 256)
            ours = rhs_ref[tile, :, at]
            theirs = rhs_ref[tile, :, width + part * 256 : width + (part + 1) * 256]
            spread = jnp.dot(gap, ours, preferred_element_type=F32)
            cos_col = jnp.dot(gap, theirs, preferred_element_type=F32)
            value = jnp.maximum(cos_col, 0.0) * pl.reciprocal(spread * spread, approx=True)
            for g in range(GROUP):
                depth = depth_ref[rows[g]]
                for half in range(2):
                    lanes = slice(part * 256 + half * 128, part * 256 + (half + 1) * 128)
                    piece = jnp.maximum(near[tile, tops[g], lanes] - depth, 0.0) * value[g * TS : (g + 1) * TS, half * 128 : (half + 1) * 128]
                    total[g] = piece if total[g] is None else total[g] + piece
        return codes, total

    def some_groups(_, place):
        done = []
        for _ in range(8):
            done.append(work_on(place))
            place = following(place)
        for codes, total in done:
            for g in range(GROUP):
                tile = codes[g] // 128
                acc[tile] = acc[tile] + total[g]
        return place

    def gather(source, _):
        column_features(packed_ref, rhs_ref, source)
        return 0

    lax.fori_loop(0, packed_ref.shape[0], gather, 0)

    def faces(step, _):
        for k in range(2):
            near[step * 2 + k] = jnp.dot(face_ref[...], rhs_ref[step * 2 + k, :, :width], preferred_element_type=F32)
        return 0

    lax.fori_loop(0, rhs_ref.shape[0] // 2, faces, 0)
    lax.fori_loop(0, (total_ref[0] + 8 - 1) // 8, some_groups, (jnp.int32(0), jnp.int32(0)))

    lane = lax.broadcasted_iota(jnp.int32, (8, 128), 1)
    second = (lane // TS) % 2 == 1
    upper = lane // (2 * TS) == 1

    def fold(step, _):
        for k in range(FOLD):
            tile = step * FOLD + k
            a0, a1, a2, a3 = [acc[tile, v * 8 : v * 8 + 8] for v in range(4)]
            low = jnp.where(second, a1, a0) + pltpu.roll(jnp.where(second, a0, a1), TS, 1)
            high = jnp.where(second, a3, a2) + pltpu.roll(jnp.where(second, a2, a3), TS, 1)
            mixed = jnp.where(upper, high, low) + pltpu.roll(jnp.where(upper, low, high), 2 * TS, 1)
            out_ref[slot_ref[tile]] = mixed
        return 0

    lax.fori_loop(0, acc.shape[0] // FOLD, fold, 0)


def assemble(total, groups, units, slot, lhs, depth, face, packed, slots):
    smem = pl.BlockSpec(memory_space=pltpu.SMEM)
    vmem = pl.BlockSpec(memory_space=pltpu.VMEM)
    columns = units.shape[0] // 64 - 1
    return pl.pallas_call(
        tiles_kernel,
        in_specs=[smem] * 4 + [vmem] * 4,
        out_specs=vmem,
        out_shape=jax.ShapeDtypeStruct((slots, 8, 128), F32),
        scratch_shapes=[
            pltpu.VMEM((slot.shape[0], TS, 128), F32),
            pltpu.VMEM((columns, face.shape[0], TS * Q), F32),
            pltpu.VMEM((columns, 48, 2 * TS * Q), BF),
        ],
        compiler_params=pltpu.CompilerParams(vmem_limit_bytes=56 * 2**20),
    )(total, groups, units, slot, lhs, depth, face, packed)


def work_list(visible, quad_mask, targets, capacity):
    span, columns = visible.shape
    order = jnp.arange(targets.shape[0], dtype=jnp.int32)
    same = targets[:, None] == targets[None, :]
    rank = jnp.sum((same & (order[:, None] > order[None, :])).astype(jnp.int32), axis=1)
    slot = targets * capacity + rank
    shifts = jnp.arange(Q, dtype=jnp.int32)
    used = ((quad_mask[:, None, :] >> shifts[None, :, None]) & 1) * visible[:, None, :]
    pair = jnp.arange(span * Q, dtype=jnp.int32)
    name = order.reshape(span, columns)
    code = (name[:, None, :] * 128 + pair.reshape(span, Q)[:, :, None]).reshape(span * Q, columns)
    used = used.reshape(span * Q, columns)
    place = jnp.sum(jnp.where(pair[:, None] > pair[None, :], 1, 0)[:, :, None] * used[None], axis=1)
    count = jnp.sum(used, axis=0)
    idle = span * Q
    hit = (place[:, None, :] == pair[None, :, None]) & (used[:, None, :] > 0)
    units = jnp.sum(jnp.where(hit, code[:, None, :] - idle, 0), axis=0) + idle
    groups = jnp.maximum((count + GROUP - 1) // GROUP, 1)
    spare = jnp.full((units.shape[0],), idle, jnp.int32)
    groups = jnp.concatenate([groups, jnp.full((1,), Q, jnp.int32)])
    return jnp.sum(groups[:-1])[None], groups, jnp.concatenate([units.T.reshape(-1), spare]), slot


def pack_columns(points, weights, normals):
    span = normals.shape[1] // TS
    flat = jnp.concatenate([points, weights[None]])
    cols = flat.reshape(4, span, TS, 4, 4).transpose(1, 3, 0, 4, 2).reshape(-1, 128)
    tiled = jnp.tile(normals.reshape(3, span, 1, TS).transpose(1, 0, 2, 3), (1, 1, 4, 1)).reshape(-1, 128)
    return jnp.concatenate([cols, tiled, jnp.zeros((-(cols.shape[0] + tiled.shape[0]) % 8, 128), F32)])


def on_device(points, normals, weights, visible, quad_mask, owners):
    devices = lax.axis_size("rows") * lax.axis_size("blk")
    sources = lax.axis_size("blk")
    capacity = max(2, 2 * owners.shape[1] // devices)
    packed = pack_columns(points, weights, normals)
    spread = jnp.broadcast_to(packed[None], (sources,) + packed.shape)
    gathered = lax.all_to_all(spread, "blk", split_axis=0, concat_axis=0, tiled=True)
    lhs, depth, face = row_features(points, weights[None], normals)
    total, groups, units, slot = work_list(visible, quad_mask, owners[0, :, 0], capacity)
    out = assemble(total, groups, units, slot, lhs, depth, face, gathered, devices * capacity)
    arrived = lax.all_to_all(
        out.reshape(devices, capacity * 8, 128), ("rows", "blk"), split_axis=0, concat_axis=0, tiled=True
    )
    return arrived.reshape(devices * capacity, TS * TS)


def solution(mesh):
    placed = (
        P(None, ("rows", "blk")),
        P(None, ("rows", "blk")),
        P(("rows", "blk")),
        P(("rows", "blk"), None),
        P(("rows", "blk"), None),
        P(("rows", "blk"), None, None),
    )
    return jax.shard_map(
        on_device, mesh=mesh, in_specs=placed, out_specs=P(("rows", "blk"), None), check_vma=False
    )
```

time: 260 us -> 125 us (0.48)
  Pallas kernels: 163 us -> 58.3 us
  local copies, waits for them, and re-layouts: 26.7 us -> 11 us
  blocking collectives: 52.5 us -> 38.4 us
  other arithmetic: 6.84 us -> 3.82 us
    pallas_call x2, Pallas kernels: 163 us -> 58.3 us  [the longest x1 55.1 us: assemble(): pl.pallas_call(tiles_kernel, in_specs=[smem] * 4 + [vmem] * 4, out_specs=...]
    all_to_all x1, blocking collectives: 52.5 us -> 38.4 us  [on_device(): lax.all_to_all(out.reshape(devices, capacity * 8, 128), ('rows', 'blk'),...]
    concatenate x5 -> x6, local copies, waits for them, and re-layouts: 9.06 us -> 4.04 us  [the longest x4 3.37 us: pack_columns(): flat = jnp.concatenate([points, weights[None]])]
    reduce_precision x1 -> x0, local copies, waits for them, and re-layouts: 2.92 us -> none  [rounded(): return lax.reduce_precision(x, 8, 7)]
    another operation x1 -> x0, other arithmetic: 2.86 us -> none
  transfers between devices with their start and end apart: 1 -> 1, of which waited for: 0 -> 1; matrix products, arithmetic and copies ran while one was open for 9% -> 4% of each run, Pallas kernels for 0% -> 3%
where the time goes in v2:
time: 125 us; the launch traced here: 124 us
  Pallas kernels  58.3 us (47%)
  blocking collectives  38.4 us (31%)
  local copies, waits for them, and re-layouts  11 us (9%)
  starting transfers between devices  9.46 us (8%)
  other arithmetic  3.82 us (3%)
  waiting for transfers between devices  2.34 us (2%)
    pallas_call x1, Pallas kernels, assemble(): pl.pallas_call(tiles_kernel, in_specs=[smem] * 4 + [vmem] * 4, out_specs=...  55.1 us
    all_to_all x1, blocking collectives, on_device(): lax.all_to_all(out.reshape(devices, capacity * 8, 128), ('rows', 'blk'),...  38.4 us
    all_to_all x1, starting transfers between devices, on_device(): lax.all_to_all(spread, 'blk', split_axis=0, concat_axis=0, tiled=True)  9.46 us
    concatenate x4, local copies, waits for them, and re-layouts, pack_columns(): flat = jnp.concatenate([points, weights[None]])  3.37 us
    unnamed x20, local copies, waits for them, and re-layouts  3.29 us
    pallas_call x1, Pallas kernels, row_features(): pl.pallas_call(rows_kernel, in_specs=[vmem] * 3, out_specs=[vmem] * 3, ou...  3.27 us
  transfers between devices with their start and end apart: 1, of which 1 were waited for; matrix products, arithmetic and copies ran while one was open for 4% of the time, Pallas kernels for 3%

profile of v2, /device:TPU:1, one launch (start us, length us, event | category | flops | bytes accessed | tf_op | source)
XLA Modules:
  0.0 123.6 jit_solution(14274227176042640691)
XLA Ops:
  0.0 0.8 reshape.155
  0.8 0.1 tile.12
  0.9 1.0 concatenate.20
  1.9 0.2 copy.18
  2.1 0.0 copy-start.7
  2.1 0.0 copy-start.8
  2.1 1.8 %concatenate.19 = f32[3,4,32,4,4]{4,3,2,1,0:T(4,128)S(1)} reshape(f32[3,2048]{1,0:T(4,128)} %points_ref.1) | data formatting | bytes 49152 | tf_op jit(solution)/shard_map/concatenate | solution.py:238
  3.9 0.0 copy-start.2
  3.9 0.0 copy-start.4
  3.9 0.0 copy-start.5
  3.9 0.0 copy-start.9
  4.0 0.4 copy.17
  4.4 0.1 reshape.154
  4.5 0.1 pad.3.clone
  4.6 0.1 maximum_maximum_fusion
  4.7 0.9 broadcast_in_dim.54
  5.6 9.5 %all-to-all-start = ((f32[16,80,128]{2,1,0:T(8,128)}), f32[16,80,128]{2,1,0:T(8,128)S(1)}, u32[]{:S(2)}, u32[]{:S(2)}) async-start(f32[16,80,128]{2,1,0:T(8,128)} %broadcast_in_dim.54), calls=%async_computation | async-start | bytes 1310720 | tf_op jit(solution)/shard_map/all_to_all | solution.py:250
  15.1 0.1 shift_right_arithmetic.43
  15.1 0.0 copy-done.7
  15.1 0.0 copy-done.8
  15.2 0.1 broadcast_compare_fusion
  15.3 0.1 bitcast_multiply_fusion
  15.3 0.1 broadcast_in_dim_reshape.24
  15.4 0.1 fusion.2
  15.5 0.8 multiply_reduce_fusion
  16.3 0.7 select_reduce_fusion
  17.0 0.1 copy.16
  17.1 0.1 reshape.153
  17.1 0.0 copy-done.2
  17.1 0.0 copy-done.4
  17.1 0.0 copy-done.5
  17.2 3.3 %shard_map.64 = (bf16[65,32,48]{2,1,0:T(8,128)(2,1)S(1)}, f32[65,32,128]{2,1,0:T(8,128)S(1)}, bf16[128,48]{1,0:T(8,128)(2,1)S(1)}) custom-call(f32[3,2048]{1,0:T(4,128)S(1)} %copy-done.2, f32[1,2048]{1,0:T(1,128)S(1)} %bitcast.29, f32[3,128]{1,0:T(4,128)S(1)} %copy-done.5), custom_call_target="tpu_custom_call" | custom-call | tf_op jit(solution)/shard_map/pallas_call | solution.py:81
  20.4 0.0 copy-start
  20.4 1.0 copy-done
  21.4 0.0 copy-start.1
  21.4 0.8 copy-done.1
  22.2 0.0 copy-start.3
  22.2 0.6 copy-done.3
  22.8 0.6 concatenate.18.units_ref
  23.4 0.6 fusion.6
  24.1 0.6 pad_add_fusion.groups_ref
  24.7 0.0 copy-done.9
  24.7 0.2 convert_reduce_fusion
  24.8 0.6 multiply_add_fusion.slot_ref
  25.4 2.3 %all-to-all-done.packed_ref = f32[16,80,128]{2,1,0:T(8,128)S(1)} async-done(((f32[16,80,128]{2,1,0:T(8,128)}), f32[16,80,128]{2,1,0:T(8,128)S(1)}, u32[]{:S(2)}, u32[]{:S(2)}) %all-to-all-start) | async-done | bytes 655392 | tf_op jit(solution)/shard_map/all_to_all | solution.py:250
  27.7 0.0 copy-start.6
  27.7 0.9 copy-done.6
  28.6 55.1 %shard_map.65 = f32[512,8,128]{2,1,0:T(8,128)} custom-call(s32[1]{0:T(128)} %bitcast.total_ref, s32[65]{0:T(128)} %pad_add_fusion.groups_ref, s32[4160]{0:T(1024)} %concatenate.18.units_ref, s32[256]{0:T(256)} %multiply_add_fusion.slot_ref, bf16[65,32,48]{2,1,0:T(8,128)(2,1)} %copy-done.1, f32[65,32,128]{2,1,0:T(8,128)} %copy-done, ...), custom_call_target="tpu_custom_call" | custom-call | tf_op jit(solution)/shard_map/pallas_call | solution.py:199
  83.7 38.4 %all_to_all.10 = f32[128,32,128]{2,1,0:T(8,128)S(1)} all-to-all(f32[128,32,128]{2,1,0:T(8,128)} %bitcast.30), channel_id=1, replica_groups=mesh['rows'=8,'blk'=16] {'rows','blk'}, dimensions={0} | all-to-all | bytes 4194304 | tf_op jit(solution)/shard_map/all_to_all | solution.py:254
  122.1 1.5 %reshape.157 = f32[512,1024]{1,0:T(8,128)} reshape(f32[128,32,128]{2,1,0:T(8,128)S(1)} %all_to_all.10) | data formatting | bytes 4194304 | tf_op jit(solution)/shard_map/reshape | solution.py:257
  (11 shorter events, 0.1 us)
Async XLA Ops:
  2.1 13.1 %copy-start.7 = (s32[4,64]{1,0:T(4,128)S(1)}, s32[4,64]{1,0:T(4,128)}, u32[]{:S(2)}) copy-start(s32[4,64]{1,0:T(4,128)} %param.9) | copy-start | bytes 3076
  2.1 13.1 %copy-start.8 = (s32[4,64]{1,0:T(4,128)S(1)}, s32[4,64]{1,0:T(4,128)}, u32[]{:S(2)}) copy-start(s32[4,64]{1,0:T(4,128)} %param.10) | copy-start | bytes 3076
  3.9 13.2 %copy-start.2 = (f32[3,2048]{1,0:T(4,128)S(1)}, f32[3,2048]{1,0:T(4,128)}, u32[]{:S(2)}) copy-start(f32[3,2048]{1,0:T(4,128)} %points_ref.1) | copy-start | bytes 73732
  3.9 13.2 %copy-start.4 = (f32[2048]{0:T(1024)S(1)}, f32[2048]{0:T(1024)}, u32[]{:S(2)}) copy-start(f32[2048]{0:T(1024)} %param.8) | copy-start | bytes 24580
  3.9 13.2 %copy-start.5 = (f32[3,128]{1,0:T(4,128)S(1)}, f32[3,128]{1,0:T(4,128)}, u32[]{:S(2)}) copy-start(f32[3,128]{1,0:T(4,128)} %normals_ref.1) | copy-start | bytes 4612
  3.9 20.7 %copy-start.9 = (s32[1,256,1]{1,2,0:T(1,128)S(1)}, s32[1,256,1]{1,2,0:T(1,128)}, u32[]{:S(2)}) copy-start(s32[1,256,1]{1,2,0:T(1,128)} %param.11) | copy-start | bytes 3076
  5.6 22.2 %all-to-all-start = ((f32[16,80,128]{2,1,0:T(8,128)}), f32[16,80,128]{2,1,0:T(8,128)S(1)}, u32[]{:S(2)}, u32[]{:S(2)}) async-start(f32[16,80,128]{2,1,0:T(8,128)} %broadcast_in_dim.54), calls=%async_computation | async-start | bytes 1310720 | tf_op jit(solution)/shard_map/all_to_all | solution.py:250
  20.4 1.0 copy-start
  21.4 0.8 copy-start.1
  22.2 0.6 copy-start.3
  27.7 0.9 copy-start.6

commit v3 on v2

--- a/solution.py
+++ b/solution.py
@@ -11,7 +11,8 @@
 Q = 16
 TS = 32
 GROUP = 4
-FOLD = 16
+FOLD = 32
+DEEP = 32
 softening = 0.05
 BF = jnp.bfloat16
 F32 = jnp.float32
@@ -36,7 +37,38 @@
     return dots[0] + dots[1] + dots[2]
 
 
-def rows_kernel(points_ref, weights_ref, normals_ref, gap_ref, depth_ref, face_ref):
+def list_work(visible_ref, mask_ref, across_ref, down_ref, capacity, total_ref, groups_ref, units_ref, slot_ref):
+    span, columns = visible_ref.shape
+    tiles = across_ref.shape[1]
+    pairs = span * Q
+    iota = lambda shape, axis: lax.broadcasted_iota(jnp.int32, shape, axis)
+    earlier = (across_ref[...] == down_ref[...]) & (iota((tiles, tiles), 0) < iota((tiles, tiles), 1))
+    rank = jnp.sum(jnp.where(earlier, 1, 0), axis=0, keepdims=True)
+    slot_ref[...] = across_ref[...] * capacity + rank
+    point = iota((Q, columns), 0)
+    used = jnp.concatenate(
+        [((mask_ref[top : top + 1] >> point) & 1) * visible_ref[top : top + 1] for top in range(span)], axis=0
+    )
+    before = jnp.where(iota((pairs, pairs), 1) < iota((pairs, pairs), 0), 1.0, 0.0).astype(BF)
+    place = jnp.dot(before, used.astype(F32).astype(BF), preferred_element_type=F32).astype(jnp.int32)
+    place = jnp.where(used > 0, place, -1)
+    count = jnp.sum(used, axis=0, keepdims=True)
+    at = iota((pairs, columns), 0)
+    column = iota((1, columns), 1)
+    units = jnp.full((pairs, columns), pairs, jnp.int32)
+    for pair in range(pairs):
+        code = (column + pair // Q * columns) * 128 + pair
+        units = jnp.where(place[pair : pair + 1] == at, code, units)
+    units_ref[...] = jnp.concatenate([units, jnp.full((pairs, 128 - columns), pairs, jnp.int32)], axis=1)
+    groups = jnp.maximum((count + GROUP - 1) // GROUP, 1)
+    groups_ref[...] = jnp.concatenate([groups, jnp.full((1, 128 - columns), Q, jnp.int32)], axis=1)
+    total_ref[...] = jnp.sum(groups, axis=1, keepdims=True)
+
+
+def prepare_kernel(
+    capacity, points_ref, weights_ref, normals_ref, visible_ref, mask_ref, across_ref, down_ref,
+    total_ref, groups_ref, units_ref, slot_ref, gap_ref, depth_ref, face_ref,
+):
     width = TS * Q
     span = normals_ref.shape[1] // TS
     iota = lambda shape, axis: lax.broadcasted_iota(jnp.int32, shape, axis)
@@ -71,24 +103,31 @@
         parts = [jnp.broadcast_to(part, (128, width)).astype(BF) for part in split(depth)]
         deep = [lax.dot_general(order, part, (across, ((), ())), preferred_element_type=F32) for part in parts]
         depth_ref[top * Q : (top + 1) * Q] = (deep[0] + deep[1] + deep[2]).reshape(Q, TS, 128)
+    list_work(visible_ref, mask_ref, across_ref, down_ref, capacity, total_ref, groups_ref, units_ref, slot_ref)
     gap_ref[span * Q] = jnp.where(iota((TS, 48), 1) == 4, 1.0, 0.0).astype(BF)
     depth_ref[span * Q] = jnp.zeros((TS, 128), F32)
 
 
-def row_features(points, weights, normals):
+def prepare(points, weights, normals, visible, quad_mask, owners, capacity):
     vmem = pl.BlockSpec(memory_space=pltpu.VMEM)
-    pairs = normals.shape[1] // TS * Q + 1
+    pairs = normals.shape[1] // TS * Q
+    tiles = owners.shape[0]
+    whole = lambda *shape: jax.ShapeDtypeStruct(shape, jnp.int32)
     return pl.pallas_call(
-        rows_kernel,
-        in_specs=[vmem] * 3,
-        out_specs=[vmem] * 3,
+        functools.partial(prepare_kernel, capacity),
+        in_specs=[vmem] * 7,
+        out_specs=[vmem] * 7,
         out_shape=[
-            jax.ShapeDtypeStruct((pairs, TS, 48), BF),
-            jax.ShapeDtypeStruct((pairs, TS, 128), F32),
+            whole(1, 1),
+            whole(1, 128),
+            whole(pairs, 128),
+            whole(1, tiles),
+            jax.ShapeDtypeStruct((pairs + 1, TS, 48), BF),
+            jax.ShapeDtypeStruct((pairs + 1, TS, 128), F32),
             jax.ShapeDtypeStruct((normals.shape[1], 48), BF),
         ],
         compiler_params=pltpu.CompilerParams(vmem_limit_bytes=40 * 2**20),
-    )(points, weights, normals)
+    )(points, weights, normals, visible, quad_mask, owners.reshape(1, tiles), owners.reshape(tiles, 1))
 
 
 def column_features(packed_ref, rhs_ref, source):
@@ -121,11 +160,11 @@
 
     def codes_of(place):
         tile, at = place
-        return [units_ref[tile * 64 + at * GROUP + g] for g in range(GROUP)]
+        return [units_ref[at * GROUP + g, tile] for g in range(GROUP)]
 
     def following(place):
         tile, at = place
-        done = at + 1 >= groups_ref[tile]
+        done = at + 1 >= groups_ref[0, tile]
         return (jnp.where(done, tile + 1, tile), jnp.where(done, 0, at + 1))
 
     def work_on(place):
@@ -151,11 +190,9 @@
         return codes, total
 
     def some_groups(_, place):
-        done = []
-        for _ in range(8):
-            done.append(work_on(place))
+        for _ in range(DEEP):
+            codes, total = work_on(place)
             place = following(place)
-        for codes, total in done:
             for g in range(GROUP):
                 tile = codes[g] // 128
                 acc[tile] = acc[tile] + total[g]
@@ -168,12 +205,12 @@
     lax.fori_loop(0, packed_ref.shape[0], gather, 0)
 
     def faces(step, _):
-        for k in range(2):
-            near[step * 2 + k] = jnp.dot(face_ref[...], rhs_ref[step * 2 + k, :, :width], preferred_element_type=F32)
+        for k in range(8):
+            near[step * 8 + k] = jnp.dot(face_ref[...], rhs_ref[step * 8 + k, :, :width], preferred_element_type=F32)
         return 0
 
-    lax.fori_loop(0, rhs_ref.shape[0] // 2, faces, 0)
-    lax.fori_loop(0, (total_ref[0] + 8 - 1) // 8, some_groups, (jnp.int32(0), jnp.int32(0)))
+    lax.fori_loop(0, rhs_ref.shape[0] // 8, faces, 0)
+    lax.fori_loop(0, (total_ref[0, 0] + DEEP - 1) // DEEP, some_groups, (jnp.int32(0), jnp.int32(0)))
 
     lane = lax.broadcasted_iota(jnp.int32, (8, 128), 1)
     second = (lane // TS) % 2 == 1
@@ -186,7 +223,7 @@
             low = jnp.where(second, a1, a0) + pltpu.roll(jnp.where(second, a0, a1), TS, 1)
             high = jnp.where(second, a3, a2) + pltpu.roll(jnp.where(second, a2, a3), TS, 1)
             mixed = jnp.where(upper, high, low) + pltpu.roll(jnp.where(upper, low, high), 2 * TS, 1)
-            out_ref[slot_ref[tile]] = mixed
+            out_ref[slot_ref[0, tile]] = mixed
         return 0
 
     lax.fori_loop(0, acc.shape[0] // FOLD, fold, 0)
@@ -195,14 +232,15 @@
 def assemble(total, groups, units, slot, lhs, depth, face, packed, slots):
     smem = pl.BlockSpec(memory_space=pltpu.SMEM)
     vmem = pl.BlockSpec(memory_space=pltpu.VMEM)
-    columns = units.shape[0] // 64 - 1
+    tiles = slot.shape[1]
+    columns = tiles * TS // face.shape[0]
     return pl.pallas_call(
         tiles_kernel,
         in_specs=[smem] * 4 + [vmem] * 4,
         out_specs=vmem,
         out_shape=jax.ShapeDtypeStruct((slots, 8, 128), F32),
         scratch_shapes=[
-            pltpu.VMEM((slot.shape[0], TS, 128), F32),
+            pltpu.VMEM((tiles, TS, 128), F32),
             pltpu.VMEM((columns, face.shape[0], TS * Q), F32),
             pltpu.VMEM((columns, 48, 2 * TS * Q), BF),
         ],
@@ -210,47 +248,52 @@
     )(total, groups, units, slot, lhs, depth, face, packed)
 
 
-def work_list(visible, quad_mask, targets, capacity):
-    span, columns = visible.shape
-    order = jnp.arange(targets.shape[0], dtype=jnp.int32)
-    same = targets[:, None] == targets[None, :]
-    rank = jnp.sum((same & (order[:, None] > order[None, :])).astype(jnp.int32), axis=1)
-    slot = targets * capacity + rank
-    shifts = jnp.arange(Q, dtype=jnp.int32)
-    used = ((quad_mask[:, None, :] >> shifts[None, :, None]) & 1) * visible[:, None, :]
-    pair = jnp.arange(span * Q, dtype=jnp.int32)
-    name = order.reshape(span, columns)
-    code = (name[:, None, :] * 128 + pair.reshape(span, Q)[:, :, None]).reshape(span * Q, columns)
-    used = used.reshape(span * Q, columns)
-    place = jnp.sum(jnp.where(pair[:, None] > pair[None, :], 1, 0)[:, :, None] * used[None], axis=1)
-    count = jnp.sum(used, axis=0)
-    idle = span * Q
-    hit = (place[:, None, :] == pair[None, :, None]) & (used[:, None, :] > 0)
-    units = jnp.sum(jnp.where(hit, code[:, None, :] - idle, 0), axis=0) + idle
-    groups = jnp.maximum((count + GROUP - 1) // GROUP, 1)
-    spare = jnp.full((units.shape[0],), idle, jnp.int32)
-    groups = jnp.concatenate([groups, jnp.full((1,), Q, jnp.int32)])
-    return jnp.sum(groups[:-1])[None], groups, jnp.concatenate([units.T.reshape(-1), spare]), slot
-
-
-def pack_columns(points, weights, normals):
-    span = normals.shape[1] // TS
-    flat = jnp.concatenate([points, weights[None]])
-    cols = flat.reshape(4, span, TS, 4, 4).transpose(1, 3, 0, 4, 2).reshape(-1, 128)
-    tiled = jnp.tile(normals.reshape(3, span, 1, TS).transpose(1, 0, 2, 3), (1, 1, 4, 1)).reshape(-1, 128)
-    return jnp.concatenate([cols, tiled, jnp.zeros((-(cols.shape[0] + tiled.shape[0]) % 8, 128), F32)])
+def pack_kernel(points_ref, weights_ref, normals_ref, out_ref, held):
+    width = TS * Q
+    span = normals_ref.shape[1] // TS
+    lane = lax.broadcasted_iota(jnp.int32, (1, width), 1)
+    wanted = (lane % TS) * Q + lane // TS
+    order = jnp.where(lax.broadcasted_iota(jnp.int32, (width, width), 0) == wanted, 1.0, 0.0).astype(BF)
+    rows = []
+    for tile in range(span):
+        at = slice(tile * width, (tile + 1) * width)
+        rows += [points_ref[:, at], weights_ref[:, at]]
+    rows = exact_dot(split(jnp.concatenate(rows, axis=0)), order)
+    held[...] = jnp.zeros_like(held)
+    for tile in range(span):
+        for lanes in range(width // 128):
+            at = tile * Q + lanes * 4
+            held[at : at + 4] = rows[tile * 4 : tile * 4 + 4, lanes * 128 : (lanes + 1) * 128]
+        normal = normals_ref[:, tile * TS : (tile + 1) * TS]
+        at = span * Q + tile * 3
+        held[at : at + 3] = jnp.concatenate([normal] * 4, axis=1)
+    for receiver in range(out_ref.shape[0]):
+        out_ref[receiver] = held[...]
+
+
+def pack_columns(points, weights, normals, receivers):
+    vmem = pl.BlockSpec(memory_space=pltpu.VMEM)
+    rows = normals.shape[1] // TS * (Q + 3)
+    rows += -rows % 8
+    return pl.pallas_call(
+        pack_kernel,
+        in_specs=[vmem] * 3,
+        out_specs=vmem,
+        out_shape=jax.ShapeDtypeStruct((receivers, rows, 128), F32),
+        scratch_shapes=[pltpu.VMEM((rows, 128), F32)],
+        compiler_params=pltpu.CompilerParams(vmem_limit_bytes=40 * 2**20),
+    )(points, weights, normals)
 
 
 def on_device(points, normals, weights, visible, quad_mask, owners):
     devices = lax.axis_size("rows") * lax.axis_size("blk")
     sources = lax.axis_size("blk")
     capacity = max(2, 2 * owners.shape[1] // devices)
-    packed = pack_columns(points, weights, normals)
-    spread = jnp.broadcast_to(packed[None], (sources,) + packed.shape)
+    weights = weights[None]
+    spread = pack_columns(points, weights, normals, sources)
     gathered = lax.all_to_all(spread, "blk", split_axis=0, concat_axis=0, tiled=True)
-    lhs, depth, face = row_features(points, weights[None], normals)
-    total, groups, units, slot = work_list(visible, quad_mask, owners[0, :, 0], capacity)
-    out = assemble(total, groups, units, slot, lhs, depth, face, gathered, devices * capacity)
+    ready = prepare(points, weights, normals, visible, quad_mask, owners[0, :, 0], capacity)
+    out = assemble(*ready, gathered, devices * capacity)
     arrived = lax.all_to_all(
         out.reshape(devices, capacity * 8, 128), ("rows", "blk"), split_axis=0, concat_axis=0, tiled=True
     )

time: 125 us -> 112 us (0.90)
  Pallas kernels: 58.3 us -> 49.8 us
  other arithmetic: 3.82 us -> 0 us
  local copies, waits for them, and re-layouts: 11 us -> 9.46 us
  waiting for transfers between devices: 2.34 us -> 3.71 us
    pallas_call x1, Pallas kernels: 55.1 us -> 44.6 us  [assemble(): pl.pallas_call(tiles_kernel, in_specs=[smem] * 4 + [vmem] * 4, out_specs=...]
    concatenate x6 -> x0, local copies, waits for them, and re-layouts: 4.04 us -> none  [the longest x4 3.37 us: pack_columns(): flat = jnp.concatenate([points, weights[None]])]
    unnamed x20 -> x32, local copies, waits for them, and re-layouts: 3.29 us -> 7.18 us
    reduce_sum x5 -> x0, other arithmetic: 2.29 us -> none  [the longest x1 0.76 us: work_list(): jnp.sum(jnp.where(pair[:, None] > pair[None, :], 1, 0)[:, :, None] * used...]
    pallas_call x1 -> x2, Pallas kernels: 3.27 us -> 5.21 us  [the longest x1 3.99 us: prepare(): pl.pallas_call(functools.partial(prepare_kernel, capacity), in_specs=[vme...]
    all_to_all x1, waiting for transfers between devices: 2.34 us -> 3.71 us  [on_device(): lax.all_to_all(spread, 'blk', split_axis=0, concat_axis=0, tiled=True)]
  transfers between devices with their start and end apart: 1 -> 1, of which waited for: 1 -> 1; matrix products, arithmetic and copies ran while one was open for 4% -> 1% of each run, Pallas kernels for 3% -> 4%
where the time goes in v3:
time: 112 us; the launch traced here: 111 us
  Pallas kernels  49.8 us (44%)
  blocking collectives  38.6 us (34%)
  local copies, waits for them, and re-layouts  9.46 us (8%)
  starting transfers between devices  9.46 us (8%)
  waiting for transfers between devices  3.71 us (3%)
    pallas_call x1, Pallas kernels, assemble(): pl.pallas_call(tiles_kernel, in_specs=[smem] * 4 + [vmem] * 4, out_specs=...  44.6 us
    all_to_all x1, blocking collectives, on_device(): lax.all_to_all(out.reshape(devices, capacity * 8, 128), ('rows', 'blk'),...  38.6 us
    all_to_all x1, starting transfers between devices, on_device(): lax.all_to_all(spread, 'blk', split_axis=0, concat_axis=0, tiled=True)  9.46 us
    unnamed x32, local copies, waits for them, and re-layouts  7.18 us
    pallas_call x1, Pallas kernels, prepare(): pl.pallas_call(functools.partial(prepare_kernel, capacity), in_specs=[vme...  3.99 us
    all_to_all x1, waiting for transfers between devices, on_device(): lax.all_to_all(spread, 'blk', split_axis=0, concat_axis=0, tiled=True)  3.71 us
  transfers between devices with their start and end apart: 1, of which 1 were waited for; matrix products, arithmetic and copies ran while one was open for 1% of the time, Pallas kernels for 4%

profile of v3, /device:TPU:1, one launch (start us, length us, event | category | flops | bytes accessed | tf_op | source)
XLA Modules:
  0.0 111.0 jit_solution(8924729748414514893)
XLA Ops:
  0.0 0.0 copy-start.10
  0.0 0.0 copy-start.2
  0.0 0.8 copy-done.2
  0.8 0.0 copy-start.6
  0.8 0.7 copy-done.6
  1.5 0.0 copy-start.8
  1.5 0.7 copy-done.8
  2.2 0.0 copy-start.3
  2.2 0.0 copy-start.7
  2.2 0.0 copy-start.9
  2.2 0.0 copy-start.11
  2.2 0.0 copy-start.12
  2.2 1.2 %shard_map.65 = f32[16,80,128]{2,1,0:T(8,128)} custom-call(f32[3,2048]{1,0:T(4,128)S(1)} %copy-done.2, f32[1,2048]{1,0:T(1,128)S(1)} %bitcast.4, f32[3,128]{1,0:T(4,128)S(1)} %copy-done.8), custom_call_target="tpu_custom_call" | custom-call | tf_op jit(solution)/shard_map/pallas_call | solution.py:278
  3.4 9.5 %all-to-all-start = ((f32[16,80,128]{2,1,0:T(8,128)}), f32[16,80,128]{2,1,0:T(8,128)S(1)}, u32[]{:S(2)}, u32[]{:S(2)}) async-start(f32[16,80,128]{2,1,0:T(8,128)} %shard_map.65), calls=%async_computation | async-start | bytes 1310720 | tf_op jit(solution)/shard_map/all_to_all | solution.py:294
  12.9 0.8 copy.7.down_ref
  13.7 0.0 copy-done.10
  13.7 0.0 copy-done.3
  13.7 0.0 copy-done.7
  13.7 0.0 copy-done.9
  13.7 0.0 copy-done.11
  13.7 0.0 copy-done.12
  13.7 4.0 %shard_map.64 = (s32[1,1]{1,0:T(1,128)}, s32[1,128]{1,0:T(1,128)S(1)}, s32[64,128]{1,0:T(8,128)S(1)}, s32[1,256]{1,0:T(1,128)S(1)}, bf16[65,32,48]{2,1,0:T(8,128...) custom-call(f32[3,2048]{1,0:T(4,128)S(1)} %copy-done.3, f32[1,2048]{1,0:T(1,128)S(1)} %bitcast.5, ...), custom_call_target="tpu_custom_call" | custom-call | tf_op jit(solution)/shard_map/pallas_call | solution.py:116
  17.7 0.0 copy-start
  17.7 1.0 copy-done
  18.7 0.0 copy-start.1
  18.7 0.8 copy-done.1
  19.5 0.0 copy-start.4
  19.5 0.6 copy-done.4
  20.1 0.0 copy-start.5
  20.1 0.6 copy-done.5
  20.7 0.0 copy-start.13
  20.7 0.6 copy-done.13
  21.3 0.0 copy-start.14
  21.3 0.6 copy-done.14
  21.9 3.7 %all-to-all-done.packed_ref = f32[16,80,128]{2,1,0:T(8,128)S(1)} async-done(((f32[16,80,128]{2,1,0:T(8,128)}), f32[16,80,128]{2,1,0:T(8,128)S(1)}, u32[]{:S(2)}, u32[]{:S(2)}) %all-to-all-start) | async-done | bytes 655392 | tf_op jit(solution)/shard_map/all_to_all | solution.py:294
  25.6 0.0 copy-start.15
  25.6 0.9 copy-done.15
  26.4 44.6 %shard_map.66 = f32[512,8,128]{2,1,0:T(8,128)} custom-call(s32[1,1]{1,0:T(1,128)} %get-tuple-element.12.total_ref, s32[1,128]{1,0:T(1,128)} %copy-done.14, s32[64,128]{1,0:T(8,128)} %copy-done.4, s32[1,256]{1,0:T(1,128)} %copy-done.13, bf16[65,32,48]{2,1,0:T(8,128)(2,1)} %copy-done.1, f32[65,32,128]{2,1,0:T(8,128)} %copy-done, bf16[128,48]{1,0:T(8,128)(2,1)} %copy-done.5, ...), custom_call_target="tpu_custom_call" | custom-call | tf_op jit(solution)/shard_map/pallas_call | solution.py:237
  71.0 38.6 %all_to_all.10 = f32[128,32,128]{2,1,0:T(8,128)S(1)} all-to-all(f32[128,32,128]{2,1,0:T(8,128)} %bitcast.8), channel_id=1, replica_groups=mesh['rows'=8,'blk'=16] {'rows','blk'}, dimensions={0} | all-to-all | bytes 4194304 | tf_op jit(solution)/shard_map/all_to_all | solution.py:297
  109.6 1.5 %reshape.7 = f32[512,1024]{1,0:T(8,128)} reshape(f32[128,32,128]{2,1,0:T(8,128)S(1)} %all_to_all.10) | data formatting | bytes 4194304 | tf_op jit(solution)/shard_map/reshape | solution.py:300
Async XLA Ops:
  0.0 13.7 %copy-start.10 = (s32[1,256,1]{1,2,0:T(1,128)S(1)}, s32[1,256,1]{1,2,0:T(1,128)}, u32[]{:S(2)}) copy-start(s32[1,256,1]{1,2,0:T(1,128)} %param.11) | copy-start | bytes 3076
  0.0 0.8 copy-start.2
  0.8 0.7 copy-start.6
  1.5 0.7 copy-start.8
  2.2 11.5 %copy-start.3 = (f32[3,2048]{1,0:T(4,128)S(1)}, f32[3,2048]{1,0:T(4,128)}, u32[]{:S(2)}) copy-start(f32[3,2048]{1,0:T(4,128)} %points_ref.3) | copy-start | bytes 73732
  2.2 11.5 %copy-start.7 = (f32[2048]{0:T(1024)S(1)}, f32[2048]{0:T(1024)}, u32[]{:S(2)}) copy-start(f32[2048]{0:T(1024)} %param.8) | copy-start | bytes 24580
  2.2 11.5 %copy-start.9 = (f32[3,128]{1,0:T(4,128)S(1)}, f32[3,128]{1,0:T(4,128)}, u32[]{:S(2)}) copy-start(f32[3,128]{1,0:T(4,128)} %normals_ref.3) | copy-start | bytes 4612
  2.2 11.6 %copy-start.11 = (s32[4,64]{1,0:T(4,128)S(1)}, s32[4,64]{1,0:T(4,128)}, u32[]{:S(2)}) copy-start(s32[4,64]{1,0:T(4,128)} %visible_ref.1) | copy-start | bytes 3076
  2.2 11.6 %copy-start.12 = (s32[4,64]{1,0:T(4,128)S(1)}, s32[4,64]{1,0:T(4,128)}, u32[]{:S(2)}) copy-start(s32[4,64]{1,0:T(4,128)} %mask_ref.1) | copy-start | bytes 3076
  3.4 22.2 %all-to-all-start = ((f32[16,80,128]{2,1,0:T(8,128)}), f32[16,80,128]{2,1,0:T(8,128)S(1)}, u32[]{:S(2)}, u32[]{:S(2)}) async-start(f32[16,80,128]{2,1,0:T(8,128)} %shard_map.65), calls=%async_computation | async-start | bytes 1310720 | tf_op jit(solution)/shard_map/all_to_all | solution.py:294
  17.7 1.0 copy-start
  18.7 0.8 copy-start.1
  19.5 0.6 copy-start.4
  20.1 0.6 copy-start.5
  20.7 0.6 copy-start.13
  21.3 0.6 copy-start.14
  25.6 0.9 copy-start.15

commit v4 on v3

--- a/solution.py
+++ b/solution.py
@@ -23,6 +23,19 @@
     rest = x - high
     middle = rest.astype(BF).astype(F32)
     return high, middle, rest - middle
+
+
+def left_rows(four, last):
+    high, middle, low = split(four)
+    tail = jnp.concatenate(list(split(last)) + [jnp.zeros((5, four.shape[1]), F32)], axis=0)
+    return jnp.concatenate([high, middle, low, high, middle, high, tail], axis=0).astype(BF)
+
+
+def right_rows(twice, ones):
+    high, middle, low = split(twice)
+    upper = lax.broadcasted_iota(jnp.int32, twice.shape, 0) < 4
+    blocks = [high, jnp.where(upper, high, middle), jnp.where(upper, middle, low), ones]
+    return jnp.concatenate(blocks, axis=0).astype(BF)
 
 
 def by_rows(shape, values, axis=0):
@@ -85,26 +98,24 @@
         x, y, z = (points_ref[k : k + 1, at] for k in range(3))
         weight = weights_ref[:, at]
         normal = normals_ref[:, top * TS : (top + 1) * TS]
-        normal = jnp.concatenate([normal, jnp.zeros((5, TS), F32)], axis=0)
-        high, middle, low = split(normal)
-        face = jnp.concatenate([high, middle, low, high, middle, high], axis=0).astype(BF)
+        normal = jnp.concatenate([normal, jnp.zeros((1, TS), F32)], axis=0)
+        face = left_rows(normal, jnp.zeros((1, TS), F32))
         face = lax.dot_general(shuffle, face, (across, ((), ())), preferred_element_type=F32)
         face_ref[top * TS : (top + 1) * TS] = face.astype(BF)
-        wide = exact_dot((high, middle, low), widen)
+        wide = exact_dot(split(normal), widen)
         depth = wide[0:1] * x + wide[1:2] * y + wide[2:3] * z
         area = exact_dot(split(jnp.broadcast_to(weight, (8, width))), same)[0:1]
         scale = area / weight
         square = x * x + y * y + z * z + softening
-        gap = by_rows((8, width), [-2.0 * x * scale, -2.0 * y * scale, -2.0 * z * scale, scale, square * scale])
-        high, middle, low = split(gap)
-        gap = jnp.concatenate([high, middle, low, high, middle, high], axis=0).astype(BF)
+        gap = jnp.concatenate([-2.0 * x * scale, -2.0 * y * scale, -2.0 * z * scale, scale], axis=0)
+        gap = left_rows(gap, square * scale)
         gap = lax.dot_general(order, gap, (across, ((), ())), preferred_element_type=F32)
-        gap_ref[top * Q : (top + 1) * Q] = gap.astype(BF).reshape(Q, TS, 48)
+        gap_ref[top * Q : (top + 1) * Q] = gap.astype(BF).reshape(Q, TS, 32)
         parts = [jnp.broadcast_to(part, (128, width)).astype(BF) for part in split(depth)]
         deep = [lax.dot_general(order, part, (across, ((), ())), preferred_element_type=F32) for part in parts]
         depth_ref[top * Q : (top + 1) * Q] = (deep[0] + deep[1] + deep[2]).reshape(Q, TS, 128)
     list_work(visible_ref, mask_ref, across_ref, down_ref, capacity, total_ref, groups_ref, units_ref, slot_ref)
-    gap_ref[span * Q] = jnp.where(iota((TS, 48), 1) == 4, 1.0, 0.0).astype(BF)
+    gap_ref[span * Q] = jnp.where(iota((TS, 32), 1) == 24, 1.0, 0.0).astype(BF)
     depth_ref[span * Q] = jnp.zeros((TS, 128), F32)
 
 
@@ -122,17 +133,18 @@
             whole(1, 128),
             whole(pairs, 128),
             whole(1, tiles),
-            jax.ShapeDtypeStruct((pairs + 1, TS, 48), BF),
+            jax.ShapeDtypeStruct((pairs + 1, TS, 32), BF),
             jax.ShapeDtypeStruct((pairs + 1, TS, 128), F32),
-            jax.ShapeDtypeStruct((normals.shape[1], 48), BF),
+            jax.ShapeDtypeStruct((normals.shape[1], 32), BF),
         ],
-        compiler_params=pltpu.CompilerParams(vmem_limit_bytes=40 * 2**20),
+        compiler_params=pltpu.CompilerParams(vmem_limit_bytes=60 * 2**20),
     )(points, weights, normals, visible, quad_mask, owners.reshape(1, tiles), owners.reshape(tiles, 1))
 
 
 def column_features(packed_ref, rhs_ref, source):
     width = TS * Q
     span = rhs_ref.shape[0] // packed_ref.shape[0]
+    ones = jnp.where(lax.broadcasted_iota(jnp.int32, (8, 128), 0) < 3, 1.0, 0.0)
     for tile in range(span):
         base = span * Q + tile * 3
         nx, ny, nz = (packed_ref[source, base + k : base + k + 1] for k in range(3))
@@ -143,13 +155,11 @@
             depth = nx * x + ny * y + nz * z
             scale = w * (1.0 / math.pi)
             half = scale * -0.5
-            ours = by_rows((8, 128), [x, y, z, square, jnp.ones_like(x)])
-            theirs = by_rows((8, 128), [nx * half, ny * half, nz * half, -depth * scale])
-            for block, start in ((ours, lanes * 128), (theirs, width + lanes * 128)):
-                high, middle, low = split(block)
-                rhs_ref[source * span + tile, :, start : start + 128] = jnp.concatenate(
-                    [high, high, high, middle, middle, low], axis=0
-                ).astype(BF)
+            four = [x, y, z, square]
+            rhs_ref[source * span + tile, :, lanes * 128 : (lanes + 1) * 128] = right_rows(by_rows((8, 128), four + four), ones)
+            four = [nx * half, ny * half, nz * half, -depth * scale]
+            start = width + lanes * 128
+            rhs_ref[source * span + tile, :, start : start + 128] = right_rows(by_rows((8, 128), four + four), ones * 0.0)
 
 
 def tiles_kernel(total_ref, groups_ref, units_ref, slot_ref, lhs_ref, depth_ref, face_ref, packed_ref, out_ref, acc, near, rhs_ref):
@@ -242,9 +252,9 @@
         scratch_shapes=[
             pltpu.VMEM((tiles, TS, 128), F32),
             pltpu.VMEM((columns, face.shape[0], TS * Q), F32),
-            pltpu.VMEM((columns, 48, 2 * TS * Q), BF),
+            pltpu.VMEM((columns, 32, 2 * TS * Q), BF),
         ],
-        compiler_params=pltpu.CompilerParams(vmem_limit_bytes=56 * 2**20),
+        compiler_params=pltpu.CompilerParams(vmem_limit_bytes=60 * 2**20),
     )(total, groups, units, slot, lhs, depth, face, packed)
 
 
@@ -281,7 +291,7 @@
         out_specs=vmem,
         out_shape=jax.ShapeDtypeStruct((receivers, rows, 128), F32),
         scratch_shapes=[pltpu.VMEM((rows, 128), F32)],
-        compiler_params=pltpu.CompilerParams(vmem_limit_bytes=40 * 2**20),
+        compiler_params=pltpu.CompilerParams(vmem_limit_bytes=60 * 2**20),
     )(points, weights, normals)
 
 

time: 112 us -> 110 us (0.982)
  local copies, waits for them, and re-layouts: 9.46 us -> 3.8 us
  Pallas kernels: 49.8 us -> 51.9 us
  waiting for transfers between devices: 3.71 us -> 5.67 us
    unnamed x32 -> x2, local copies, waits for them, and re-layouts: 7.18 us -> 0.86 us
    all_to_all x1, waiting for transfers between devices: 3.71 us -> 5.67 us  [on_device(): lax.all_to_all(spread, 'blk', split_axis=0, concat_axis=0, tiled=True)]
    pallas_call x1, Pallas kernels: 3.99 us -> 5.57 us  [prepare(): pl.pallas_call(functools.partial(prepare_kernel, capacity), in_specs=[vme...]
  transfers between devices with their start and end apart: 1 -> 1, of which waited for: 1 -> 1; matrix products, arithmetic and copies ran while one was open for 1% -> 1% of each run, Pallas kernels for 4% -> 5%
where the time goes in v4:
time: 110 us; the launch traced here: 109 us
  Pallas kernels  51.9 us (47%)
  blocking collectives  38.6 us (35%)
  starting transfers between devices  9.46 us (9%)
  waiting for transfers between devices  5.67 us (5%)
  local copies, waits for them, and re-layouts  3.8 us (3%)
    pallas_call x1, Pallas kernels, assemble(): pl.pallas_call(tiles_kernel, in_specs=[smem] * 4 + [vmem] * 4, out_specs=...  44.4 us
    all_to_all x1, blocking collectives, on_device(): lax.all_to_all(out.reshape(devices, capacity * 8, 128), ('rows', 'blk'),...  38.6 us
    all_to_all x1, starting transfers between devices, on_device(): lax.all_to_all(spread, 'blk', split_axis=0, concat_axis=0, tiled=True)  9.46 us
    all_to_all x1, waiting for transfers between devices, on_device(): lax.all_to_all(spread, 'blk', split_axis=0, concat_axis=0, tiled=True)  5.67 us
    pallas_call x1, Pallas kernels, prepare(): pl.pallas_call(functools.partial(prepare_kernel, capacity), in_specs=[vme...  5.57 us
  transfers between devices with their start and end apart: 1, of which 1 were waited for; matrix products, arithmetic and copies ran while one was open for 1% of the time, Pallas kernels for 5%

profile of v4, /device:TPU:1, one launch (start us, length us, event | category | flops | bytes accessed | tf_op | source)
XLA Modules:
  0.0 109.5 jit_solution(13131491532851831278)
XLA Ops:
  0.0 2.0 %shard_map.65 = f32[16,80,128]{2,1,0:T(8,128)} custom-call(f32[3,2048]{1,0:T(4,128)} %points_ref.3, f32[1,2048]{1,0:T(1,128)} %bitcast.5, f32[3,128]{1,0:T(4,128)} %normals_ref.3), custom_call_target="tpu_custom_call" | custom-call | tf_op jit(solution)/shard_map/pallas_call | solution.py:288
  2.0 9.5 %all-to-all-start = ((f32[16,80,128]{2,1,0:T(8,128)}), f32[16,80,128]{2,1,0:T(8,128)S(1)}, u32[]{:S(2)}, u32[]{:S(2)}) async-start(f32[16,80,128]{2,1,0:T(8,128)} %shard_map.65), calls=%async_computation | async-start | bytes 1310720 | tf_op jit(solution)/shard_map/all_to_all | solution.py:304
  11.5 1.5 %copy.7.down_ref = s32[256,1]{1,0:T(8,128)} copy(s32[256,1]{0,1:T(1,128)} %bitcast.7) | data formatting | bytes 2048 | tf_op jit(solution)/shard_map/reshape;squeeze | solution.py:141
  12.9 5.6 %shard_map.64 = (s32[1,1]{1,0:T(1,128)}, s32[1,128]{1,0:T(1,128)}, s32[64,128]{1,0:T(8,128)}, s32[1,256]{1,0:T(1,128)}, bf16[65,32,32]{2,1,0:T(8,128)(2,1)}, /*i...) custom-call(f32[3,2048]{1,0:T(4,128)} %points_ref.3, f32[1,2048]{1,0:T(1,128)} %bitcast.6, f32[3,128]{1,0:T(4,128)} %normals_ref.3, ...), custom_call_target="tpu_custom_call" | custom-call | tf_op jit(solution)/shard_map/pallas_call | solution.py:127
  18.5 5.7 %all-to-all-done.packed_ref = f32[16,80,128]{2,1,0:T(8,128)S(1)} async-done(((f32[16,80,128]{2,1,0:T(8,128)}), f32[16,80,128]{2,1,0:T(8,128)S(1)}, u32[]{:S(2)}, u32[]{:S(2)}) %all-to-all-start) | async-done | bytes 655392 | tf_op jit(solution)/shard_map/all_to_all | solution.py:304
  24.2 0.0 copy-start
  24.2 0.9 copy-done
  25.0 44.4 %shard_map.66 = f32[512,8,128]{2,1,0:T(8,128)} custom-call(s32[1,1]{1,0:T(1,128)} %get-tuple-element.12.total_ref, s32[1,128]{1,0:T(1,128)} %get-tuple-element.13.groups_ref, s32[64,128]{1,0:T(8,128)} %get-tuple-element.14.units_ref, s32[1,256]{1,0:T(1,128)} %get-tuple-element.15.slot_ref, bf16[65,32,32]{2,1,0:T(8,128)(2,1)} %get-tuple-element.16.lhs_ref, ...), custom_call_target="tpu_custom_call" | custom-call | tf_op jit(solution)/shard_map/pallas_call | solution.py:247
  69.4 38.6 %all_to_all.10 = f32[128,32,128]{2,1,0:T(8,128)S(1)} all-to-all(f32[128,32,128]{2,1,0:T(8,128)} %bitcast.4), channel_id=1, replica_groups=mesh['rows'=8,'blk'=16] {'rows','blk'}, dimensions={0} | all-to-all | bytes 4194304 | tf_op jit(solution)/shard_map/all_to_all | solution.py:307
  108.0 1.5 %reshape.7 = f32[512,1024]{1,0:T(8,128)} reshape(f32[128,32,128]{2,1,0:T(8,128)S(1)} %all_to_all.10) | data formatting | bytes 4194304 | tf_op jit(solution)/shard_map/reshape | solution.py:310
Async XLA Ops:
  2.0 22.2 %all-to-all-start = ((f32[16,80,128]{2,1,0:T(8,128)}), f32[16,80,128]{2,1,0:T(8,128)S(1)}, u32[]{:S(2)}, u32[]{:S(2)}) async-start(f32[16,80,128]{2,1,0:T(8,128)} %shard_map.65), calls=%async_computation | async-start | bytes 1310720 | tf_op jit(solution)/shard_map/all_to_all | solution.py:304
  24.2 0.9 copy-start

commit v5 on v4

--- a/solution.py
+++ b/solution.py
@@ -12,7 +12,8 @@
 TS = 32
 GROUP = 4
 FOLD = 32
-DEEP = 32
+DEEP = 64
+REST = 8
 softening = 0.05
 BF = jnp.bfloat16
 F32 = jnp.float32
@@ -162,7 +163,17 @@
             rhs_ref[source * span + tile, :, start : start + 128] = right_rows(by_rows((8, 128), four + four), ones * 0.0)
 
 
-def tiles_kernel(total_ref, groups_ref, units_ref, slot_ref, lhs_ref, depth_ref, face_ref, packed_ref, out_ref, acc, near, rhs_ref):
+def tiles_kernel(
+    total_ref, groups_ref, units_ref, slot_ref, lhs_hbm, depth_hbm, face_hbm, packed_hbm, out_ref,
+    acc, near, rhs_ref, lhs_ref, depth_ref, face_ref, packed_ref, arrived,
+):
+    far = (packed_hbm, face_hbm, lhs_hbm, depth_hbm)
+    copies = [
+        pltpu.make_async_copy(source, target, arrived.at[k])
+        for k, (source, target) in enumerate(zip(far, (packed_ref, face_ref, lhs_ref, depth_ref)))
+    ]
+    for copy in copies:
+        copy.start()
     out_ref[...] = jnp.zeros_like(out_ref)
     acc[...] = jnp.zeros_like(acc)
     width = TS * Q
@@ -199,19 +210,23 @@
                     total[g] = piece if total[g] is None else total[g] + piece
         return codes, total
 
-    def some_groups(_, place):
-        for _ in range(DEEP):
-            codes, total = work_on(place)
-            place = following(place)
-            for g in range(GROUP):
-                tile = codes[g] // 128
-                acc[tile] = acc[tile] + total[g]
-        return place
+    def some_groups(count):
+        def run(_, place):
+            for _ in range(count):
+                codes, total = work_on(place)
+                place = following(place)
+                for g in range(GROUP):
+                    tile = codes[g] // 128
+                    acc[tile] = acc[tile] + total[g]
+            return place
+
+        return run
 
     def gather(source, _):
         column_features(packed_ref, rhs_ref, source)
         return 0
 
+    copies[0].wait()
     lax.fori_loop(0, packed_ref.shape[0], gather, 0)
 
     def faces(step, _):
@@ -219,8 +234,14 @@
             near[step * 8 + k] = jnp.dot(face_ref[...], rhs_ref[step * 8 + k, :, :width], preferred_element_type=F32)
         return 0
 
+    copies[1].wait()
     lax.fori_loop(0, rhs_ref.shape[0] // 8, faces, 0)
-    lax.fori_loop(0, (total_ref[0, 0] + DEEP - 1) // DEEP, some_groups, (jnp.int32(0), jnp.int32(0)))
+    copies[2].wait()
+    copies[3].wait()
+    whole = total_ref[0, 0] // DEEP
+    rest = total_ref[0, 0] - whole * DEEP
+    place = lax.fori_loop(0, whole, some_groups(DEEP), (jnp.int32(0), jnp.int32(0)))
+    lax.fori_loop(0, (rest + REST - 1) // REST, some_groups(REST), place)
 
     lane = lax.broadcasted_iota(jnp.int32, (8, 128), 1)
     second = (lane // TS) % 2 == 1
@@ -246,13 +267,18 @@
     columns = tiles * TS // face.shape[0]
     return pl.pallas_call(
         tiles_kernel,
-        in_specs=[smem] * 4 + [vmem] * 4,
+        in_specs=[smem] * 4 + [pl.BlockSpec(memory_space=pl.ANY)] * 4,
         out_specs=vmem,
         out_shape=jax.ShapeDtypeStruct((slots, 8, 128), F32),
         scratch_shapes=[
             pltpu.VMEM((tiles, TS, 128), F32),
             pltpu.VMEM((columns, face.shape[0], TS * Q), F32),
             pltpu.VMEM((columns, 32, 2 * TS * Q), BF),
+            pltpu.VMEM(lhs.shape, BF),
+            pltpu.VMEM(depth.shape, F32),
+            pltpu.VMEM(face.shape, BF),
+            pltpu.VMEM(packed.shape, F32),
+            pltpu.SemaphoreType.DMA((4,)),
         ],
         compiler_params=pltpu.CompilerParams(vmem_limit_bytes=60 * 2**20),
     )(total, groups, units, slot, lhs, depth, face, packed)

time: 110 us -> 110 us (level)
  Pallas kernels: 51.9 us -> 49.5 us
  blocking collectives: 38.6 us -> 40.9 us
    pallas_call x1, Pallas kernels: 44.4 us -> 42 us  [assemble(): pl.pallas_call(tiles_kernel, in_specs=[smem] * 4 + [pl.BlockSpec(memory_s...]
    all_to_all x1, blocking collectives: 38.6 us -> 40.9 us  [on_device(): lax.all_to_all(out.reshape(devices, capacity * 8, 128), ('rows', 'blk'),...]
where the time goes in v5:
time: 110 us; the launch traced here: 109 us
  Pallas kernels  49.5 us (45%)
  blocking collectives  40.9 us (37%)
  starting transfers between devices  9.46 us (9%)
  waiting for transfers between devices  5.67 us (5%)
  local copies, waits for them, and re-layouts  3.8 us (3%)
    pallas_call x1, Pallas kernels, assemble(): pl.pallas_call(tiles_kernel, in_specs=[smem] * 4 + [pl.BlockSpec(memory_s...  42 us
    all_to_all x1, blocking collectives, on_device(): lax.all_to_all(out.reshape(devices, capacity * 8, 128), ('rows', 'blk'),...  40.9 us
    all_to_all x1, starting transfers between devices, on_device(): lax.all_to_all(spread, 'blk', split_axis=0, concat_axis=0, tiled=True)  9.46 us
    all_to_all x1, waiting for transfers between devices, on_device(): lax.all_to_all(spread, 'blk', split_axis=0, concat_axis=0, tiled=True)  5.67 us
    pallas_call x1, Pallas kernels, prepare(): pl.pallas_call(functools.partial(prepare_kernel, capacity), in_specs=[vme...  5.57 us
  transfers between devices with their start and end apart: 1, of which 1 were waited for; matrix products, arithmetic and copies ran while one was open for 1% of the time, Pallas kernels for 5%

profile of v5, /device:TPU:1, one launch (start us, length us, event | category | flops | bytes accessed | tf_op | source)
XLA Modules:
  0.0 109.3 jit_solution(15382518834851277160)
XLA Ops:
  0.0 2.0 %shard_map.65 = f32[16,80,128]{2,1,0:T(8,128)} custom-call(f32[3,2048]{1,0:T(4,128)} %points_ref.3, f32[1,2048]{1,0:T(1,128)} %bitcast.5, f32[3,128]{1,0:T(4,128)} %normals_ref.3), custom_call_target="tpu_custom_call" | custom-call | tf_op jit(solution)/shard_map/pallas_call | solution.py:314
  2.0 9.5 %all-to-all-start = ((f32[16,80,128]{2,1,0:T(8,128)}), f32[16,80,128]{2,1,0:T(8,128)S(1)}, u32[]{:S(2)}, u32[]{:S(2)}) async-start(f32[16,80,128]{2,1,0:T(8,128)} %shard_map.65), calls=%async_computation | async-start | bytes 1310720 | tf_op jit(solution)/shard_map/all_to_all | solution.py:330
  11.5 1.5 %copy.7.down_ref = s32[256,1]{1,0:T(8,128)} copy(s32[256,1]{0,1:T(1,128)} %bitcast.7) | data formatting | bytes 2048 | tf_op jit(solution)/shard_map/reshape;squeeze | solution.py:142
  12.9 5.6 %shard_map.64 = (s32[1,1]{1,0:T(1,128)}, s32[1,128]{1,0:T(1,128)}, s32[64,128]{1,0:T(8,128)}, s32[1,256]{1,0:T(1,128)}, bf16[65,32,32]{2,1,0:T(8,128)(2,1)}, /*i...) custom-call(f32[3,2048]{1,0:T(4,128)} %points_ref.3, f32[1,2048]{1,0:T(1,128)} %bitcast.6, f32[3,128]{1,0:T(4,128)} %normals_ref.3, ...), custom_call_target="tpu_custom_call" | custom-call | tf_op jit(solution)/shard_map/pallas_call | solution.py:128
  18.5 5.7 %all-to-all-done.packed_hbm = f32[16,80,128]{2,1,0:T(8,128)S(1)} async-done(((f32[16,80,128]{2,1,0:T(8,128)}), f32[16,80,128]{2,1,0:T(8,128)S(1)}, u32[]{:S(2)}, u32[]{:S(2)}) %all-to-all-start) | async-done | bytes 655392 | tf_op jit(solution)/shard_map/all_to_all | solution.py:330
  24.2 0.0 copy-start
  24.2 0.9 copy-done
  25.0 42.0 %shard_map.66 = f32[512,8,128]{2,1,0:T(8,128)} custom-call(s32[1,1]{1,0:T(1,128)} %get-tuple-element.12.total_ref, s32[1,128]{1,0:T(1,128)} %get-tuple-element.13.groups_ref, s32[64,128]{1,0:T(8,128)} %get-tuple-element.14.units_ref, s32[1,256]{1,0:T(1,128)} %get-tuple-element.15.slot_ref, bf16[65,32,32]{2,1,0:T(8,128)(2,1)} %get-tuple-element.16.lhs_hbm, ...), custom_call_target="tpu_custom_call" | custom-call | tf_op jit(solution)/shard_map/pallas_call | solution.py:268
  67.0 40.9 %all_to_all.10 = f32[128,32,128]{2,1,0:T(8,128)S(1)} all-to-all(f32[128,32,128]{2,1,0:T(8,128)} %bitcast.4), channel_id=1, replica_groups=mesh['rows'=8,'blk'=16] {'rows','blk'}, dimensions={0} | all-to-all | bytes 4194304 | tf_op jit(solution)/shard_map/all_to_all | solution.py:333
  107.9 1.5 %reshape.7 = f32[512,1024]{1,0:T(8,128)} reshape(f32[128,32,128]{2,1,0:T(8,128)S(1)} %all_to_all.10) | data formatting | bytes 4194304 | tf_op jit(solution)/shard_map/reshape | solution.py:336
Async XLA Ops:
  2.0 22.2 %all-to-all-start = ((f32[16,80,128]{2,1,0:T(8,128)}), f32[16,80,128]{2,1,0:T(8,128)S(1)}, u32[]{:S(2)}, u32[]{:S(2)}) async-start(f32[16,80,128]{2,1,0:T(8,128)} %shard_map.65), calls=%async_computation | async-start | bytes 1310720 | tf_op jit(solution)/shard_map/all_to_all | solution.py:330
  24.2 0.9 copy-start

commit v6 on v5

--- a/solution.py
+++ b/solution.py
@@ -138,7 +138,7 @@
             jax.ShapeDtypeStruct((pairs + 1, TS, 128), F32),
             jax.ShapeDtypeStruct((normals.shape[1], 32), BF),
         ],
-        compiler_params=pltpu.CompilerParams(vmem_limit_bytes=60 * 2**20),
+        compiler_params=pltpu.CompilerParams(vmem_limit_bytes=40 * 2**20),
     )(points, weights, normals, visible, quad_mask, owners.reshape(1, tiles), owners.reshape(tiles, 1))
 
 
@@ -164,13 +164,13 @@
 
 
 def tiles_kernel(
-    total_ref, groups_ref, units_ref, slot_ref, lhs_hbm, depth_hbm, face_hbm, packed_hbm, out_ref,
-    acc, near, rhs_ref, lhs_ref, depth_ref, face_ref, packed_ref, arrived,
+    total_ref, groups_ref, units_ref, slot_ref, lhs_hbm, depth_hbm, face_hbm, packed_ref, out_ref,
+    acc, near, rhs_ref, lhs_ref, depth_ref, face_ref, arrived,
 ):
-    far = (packed_hbm, face_hbm, lhs_hbm, depth_hbm)
+    far = (face_hbm, lhs_hbm, depth_hbm)
     copies = [
         pltpu.make_async_copy(source, target, arrived.at[k])
-        for k, (source, target) in enumerate(zip(far, (packed_ref, face_ref, lhs_ref, depth_ref)))
+        for k, (source, target) in enumerate(zip(far, (face_ref, lhs_ref, depth_ref)))
     ]
     for copy in copies:
         copy.start()
@@ -226,7 +226,6 @@
         column_features(packed_ref, rhs_ref, source)
         return 0
 
-    copies[0].wait()
     lax.fori_loop(0, packed_ref.shape[0], gather, 0)
 
     def faces(step, _):
@@ -234,10 +233,10 @@
             near[step * 8 + k] = jnp.dot(face_ref[...], rhs_ref[step * 8 + k, :, :width], preferred_element_type=F32)
         return 0
 
+    copies[0].wait()
+    lax.fori_loop(0, rhs_ref.shape[0] // 8, faces, 0)
     copies[1].wait()
-    lax.fori_loop(0, rhs_ref.shape[0] // 8, faces, 0)
     copies[2].wait()
-    copies[3].wait()
     whole = total_ref[0, 0] // DEEP
     rest = total_ref[0, 0] - whole * DEEP
     place = lax.fori_loop(0, whole, some_groups(DEEP), (jnp.int32(0), jnp.int32(0)))
@@ -267,7 +266,7 @@
     columns = tiles * TS // face.shape[0]
     return pl.pallas_call(
         tiles_kernel,
-        in_specs=[smem] * 4 + [pl.BlockSpec(memory_space=pl.ANY)] * 4,
+        in_specs=[smem] * 4 + [pl.BlockSpec(memory_space=pl.ANY)] * 3 + [vmem],
         out_specs=vmem,
         out_shape=jax.ShapeDtypeStruct((slots, 8, 128), F32),
         scratch_shapes=[
@@ -277,10 +276,9 @@
             pltpu.VMEM(lhs.shape, BF),
             pltpu.VMEM(depth.shape, F32),
             pltpu.VMEM(face.shape, BF),
-            pltpu.VMEM(packed.shape, F32),
-            pltpu.SemaphoreType.DMA((4,)),
+            pltpu.SemaphoreType.DMA((3,)),
         ],
-        compiler_params=pltpu.CompilerParams(vmem_limit_bytes=60 * 2**20),
+        compiler_params=pltpu.CompilerParams(vmem_limit_bytes=34 * 2**20),
     )(total, groups, units, slot, lhs, depth, face, packed)
 
 

time: 110 us -> 106 us (0.964)
  blocking collectives: 40.9 us -> 37.5 us
  waiting for transfers between devices: 5.67 us -> 7.79 us
  local copies, waits for them, and re-layouts: 3.8 us -> 2.31 us
    all_to_all x1, blocking collectives: 40.9 us -> 37.5 us  [on_device(): lax.all_to_all(out.reshape(devices, capacity * 8, 128), ('rows', 'blk'),...]
    all_to_all x1, waiting for transfers between devices: 5.67 us -> 7.79 us  [on_device(): lax.all_to_all(spread, 'blk', split_axis=0, concat_axis=0, tiled=True)]
    pallas_call x1, Pallas kernels: 5.57 us -> 4.04 us  [prepare(): pl.pallas_call(functools.partial(prepare_kernel, capacity), in_specs=[vme...]
  transfers between devices with their start and end apart: 1 -> 1, of which waited for: 1 -> 1; matrix products, arithmetic and copies ran while one was open for 1% -> 1% of each run, Pallas kernels for 5% -> 4%
where the time goes in v6:
time: 106 us
  Pallas kernels  48.6 us (46%)
  blocking collectives  37.5 us (35%)
  starting transfers between devices  9.46 us (9%)
  waiting for transfers between devices  7.79 us (7%)
  local copies, waits for them, and re-layouts  2.31 us (2%)
    pallas_call x1, Pallas kernels, assemble(): pl.pallas_call(tiles_kernel, in_specs=[smem] * 4 + [pl.BlockSpec(memory_s...  42.5 us
    all_to_all x1, blocking collectives, on_device(): lax.all_to_all(out.reshape(devices, capacity * 8, 128), ('rows', 'blk'),...  37.5 us
    all_to_all x1, starting transfers between devices, on_device(): lax.all_to_all(spread, 'blk', split_axis=0, concat_axis=0, tiled=True)  9.46 us
    all_to_all x1, waiting for transfers between devices, on_device(): lax.all_to_all(spread, 'blk', split_axis=0, concat_axis=0, tiled=True)  7.79 us
    pallas_call x1, Pallas kernels, prepare(): pl.pallas_call(functools.partial(prepare_kernel, capacity), in_specs=[vme...  4.04 us
  transfers between devices with their start and end apart: 1, of which 1 were waited for; matrix products, arithmetic and copies ran while one was open for 1% of the time, Pallas kernels for 4%

profile of v6, /device:TPU:1, one launch (start us, length us, event | category | flops | bytes accessed | tf_op | source)
XLA Modules:
  0.0 105.7 jit_solution(548654923128919054)
XLA Ops:
  0.0 0.0 copy-start.2
  0.0 0.0 copy-start
  0.0 0.0 copy-start.1
  0.0 0.0 copy-start.3
  0.0 0.0 copy-start.5
  0.0 0.0 copy-start.4
  0.0 2.0 %shard_map.65 = f32[16,80,128]{2,1,0:T(8,128)} custom-call(f32[3,2048]{1,0:T(4,128)} %points_ref.3, f32[1,2048]{1,0:T(1,128)} %bitcast.5, f32[3,128]{1,0:T(4,128)} %normals_ref.3), custom_call_target="tpu_custom_call" | custom-call | tf_op jit(solution)/shard_map/pallas_call | solution.py:312
  2.1 9.5 %all-to-all-start = ((f32[16,80,128]{2,1,0:T(8,128)}), f32[16,80,128]{2,1,0:T(8,128)S(1)}, u32[]{:S(2)}, u32[]{:S(2)}) async-start(f32[16,80,128]{2,1,0:T(8,128)} %shard_map.65), calls=%async_computation | async-start | bytes 1310720 | tf_op jit(solution)/shard_map/all_to_all | solution.py:328
  11.6 0.8 copy.7.down_ref
  12.4 0.0 copy-done.2
  12.4 0.0 copy-done
  12.4 0.0 copy-done.1
  12.4 0.0 copy-done.3
  12.4 0.0 copy-done.5
  12.4 0.0 copy-done.4
  12.4 4.0 %shard_map.64 = (s32[1,1]{1,0:T(1,128)}, s32[1,128]{1,0:T(1,128)S(1)}, s32[64,128]{1,0:T(8,128)S(1)}, s32[1,256]{1,0:T(1,128)S(1)}, bf16[65,32,32]{2,1,0:T(8,128...) custom-call(f32[3,2048]{1,0:T(4,128)S(1)} %copy-done, f32[1,2048]{1,0:T(1,128)S(1)} %bitcast.6, ...), custom_call_target="tpu_custom_call" | custom-call | tf_op jit(solution)/shard_map/pallas_call | solution.py:128
  16.5 7.8 %all-to-all-done.packed_ref = f32[16,80,128]{2,1,0:T(8,128)S(1)} async-done(((f32[16,80,128]{2,1,0:T(8,128)}), f32[16,80,128]{2,1,0:T(8,128)S(1)}, u32[]{:S(2)}, u32[]{:S(2)}) %all-to-all-start) | async-done | bytes 655392 | tf_op jit(solution)/shard_map/all_to_all | solution.py:328
  24.3 42.5 %shard_map.66 = f32[512,8,128]{2,1,0:T(8,128)S(1)} custom-call(s32[1,1]{1,0:T(1,128)} %get-tuple-element.12.total_ref, s32[1,128]{1,0:T(1,128)S(1)} %get-tuple-element.13.groups_ref, s32[64,128]{1,0:T(8,128)S(1)} %get-tuple-element.14.units_ref, s32[1,256]{1,0:T(1,128)S(1)} %get-tuple-element.15.slot_ref, bf16[65,32,32]{2,1,0:T(8,128)(2,1)S(1)} %get-tuple-element.16.lhs_hbm, ...), custom_call_target="tpu_custom_call" | custom-call | tf_op jit(solution)/shard_map/pallas_call | solution.py:267
  66.7 37.5 %all_to_all.10 = f32[128,32,128]{2,1,0:T(8,128)S(1)} all-to-all(f32[128,32,128]{2,1,0:T(8,128)S(1)} %bitcast.4), channel_id=1, replica_groups=mesh['rows'=8,'blk'=16] {'rows','blk'}, dimensions={0} | all-to-all | bytes 4194304 | tf_op jit(solution)/shard_map/all_to_all | solution.py:331
  104.2 1.5 %reshape.7 = f32[512,1024]{1,0:T(8,128)} reshape(f32[128,32,128]{2,1,0:T(8,128)S(1)} %all_to_all.10) | data formatting | bytes 4194304 | tf_op jit(solution)/shard_map/reshape | solution.py:334
Async XLA Ops:
  0.0 12.4 %copy-start.2 = (f32[3,128]{1,0:T(4,128)S(1)}, f32[3,128]{1,0:T(4,128)}, u32[]{:S(2)}) copy-start(f32[3,128]{1,0:T(4,128)} %normals_ref.3) | copy-start | bytes 4612
  0.0 12.4 %copy-start = (f32[3,2048]{1,0:T(4,128)S(1)}, f32[3,2048]{1,0:T(4,128)}, u32[]{:S(2)}) copy-start(f32[3,2048]{1,0:T(4,128)} %points_ref.3) | copy-start | bytes 73732
  0.0 12.4 %copy-start.1 = (f32[2048]{0:T(1024)S(1)}, f32[2048]{0:T(1024)}, u32[]{:S(2)}) copy-start(f32[2048]{0:T(1024)} %param.8) | copy-start | bytes 24580
  0.0 12.4 %copy-start.3 = (s32[1,256,1]{1,2,0:T(1,128)S(1)}, s32[1,256,1]{1,2,0:T(1,128)}, u32[]{:S(2)}) copy-start(s32[1,256,1]{1,2,0:T(1,128)} %param.11) | copy-start | bytes 3076
  0.0 12.4 %copy-start.5 = (s32[4,64]{1,0:T(4,128)S(1)}, s32[4,64]{1,0:T(4,128)}, u32[]{:S(2)}) copy-start(s32[4,64]{1,0:T(4,128)} %mask_ref.1) | copy-start | bytes 3076
  0.0 12.4 %copy-start.4 = (s32[4,64]{1,0:T(4,128)S(1)}, s32[4,64]{1,0:T(4,128)}, u32[]{:S(2)}) copy-start(s32[4,64]{1,0:T(4,128)} %visible_ref.1) | copy-start | bytes 3076
  2.1 22.2 %all-to-all-start = ((f32[16,80,128]{2,1,0:T(8,128)}), f32[16,80,128]{2,1,0:T(8,128)S(1)}, u32[]{:S(2)}, u32[]{:S(2)}) async-start(f32[16,80,128]{2,1,0:T(8,128)} %shard_map.65), calls=%async_computation | async-start | bytes 1310720 | tf_op jit(solution)/shard_map/all_to_all | solution.py:328
